TPU v7x, 32 devices: a whole 2x2x4 slice. The times are simulated.
32 devices in a mesh: dp: 16 (over z, y, x), blk: 2 (over core).
Axes of the slice: x: 2, y: 2, z: 4, core: 2. Of those that a mesh axis runs over, the one named last changes fastest.
Arguments:
- inputs: bfloat16 [32, 256, 1152], P('dp', 'blk'), may hold values from -6 to 6
- conditioning: bfloat16 [32, 1152], P('dp'), may hold values from -6 to 6
- grid_sizes: int32 [32, 2], P('dp'), may hold values from 12 to 20, as said below
- ada_weight: bfloat16 [1152, 6912], P('blk'), may hold values from -0.1875 to 0.1875
- ada_bias: bfloat16 [6912], replicated, may hold values from -1.796875 to 1.796875
- qkv_weight: bfloat16 [1152, 3456], P('blk'), may hold values from -0.1875 to 0.1875
- qv_bias: bfloat16 [2304], replicated, may hold values from -1.796875 to 1.796875
- proj_weight: bfloat16 [1152, 1152], P('blk'), may hold values from -1.5 to 1.5
- proj_bias: bfloat16 [1152], replicated, may hold values from -1.796875 to 1.796875
- fc1_weight: bfloat16 [1152, 4608], P('blk'), may hold values from -0.1875 to 0.1875
- fc1_bias: bfloat16 [4608], replicated, may hold values from -1.796875 to 1.796875
- fc2_weight: bfloat16 [4608, 1152], P('blk'), may hold values from -0.09375 to 0.09375
- fc2_bias: bfloat16 [1152], replicated, may hold values from -1.796875 to 1.796875
- cotangent: bfloat16 [32, 256, 1152], P('dp', 'blk'), may hold values from -6 to 6
Outputs:
- output: bfloat16 [32, 256, 1152], P('dp', 'blk')
- input_grad: float32 [32, 256, 1152], P('dp', 'blk')
- cond_grad: float32 [32, 1152], P('dp')
- ada_weight_grad: float32 [1152, 6912], P('dp', 'blk')
- ada_bias_grad: float32 [6912], P('dp')
- qkv_weight_grad: float32 [1152, 3456], P('dp', 'blk')
- qv_bias_grad: float32 [2304], P('dp')
- proj_weight_grad: float32 [1152, 1152], P('dp', 'blk')
- proj_bias_grad: float32 [1152], P('dp')
- fc1_weight_grad: float32 [1152, 4608], P('dp', 'blk')
- fc1_bias_grad: float32 [4608], P('dp')
- fc2_weight_grad: float32 [4608, 1152], P('dp', 'blk')
- fc2_bias_grad: float32 [1152], P('dp')
Inputs may be any that keep to these rules, and one draw needn't show every extreme that they name: `grid_sizes`: each row holds a latent grid's height and width, whose product lies between 144 and 256; the first image's grid is 20 by 12 and the second's 12 by 20.
All inputs are finite; a program needn't handle non-finite values.
Results may differ from a plain program's by a relative error of at most 0.014.
The roundings to bfloat16 on the way count: a program that leaves them out, or rounds other values in their place, can miss the bound.
Values may be sent and summed in bfloat16 or wider, within the bound.
No kernel may reach another device: no remote copies, remote signals or barrier semaphores. Data moves between devices by JAX's collectives and lax.ppermute only.
A program may use at most 320 MiB of HBM per device.

v0:
```python
import jax
import jax.numpy as jnp
from jax import lax
from jax.sharding import PartitionSpec as P

HEADS = 16


EPS = 1e-06
MASKED = -1e30


def normalize(values_in):
    average = jnp.mean(values_in, -1, keepdims=True)
    centred = values_in - average
    return centred * lax.rsqrt(jnp.mean(centred * centred, -1, keepdims=True) + EPS)


def gelu_tanh(values_in):
    return jax.nn.gelu(values_in, approximate=True)


def transpose_product(left, right):
    return lax.dot_general(
        left, right, (((0,), (0,)), ((), ())), preferred_element_type=jnp.float32
    )


def product_back(left, right):
    return lax.dot_general(
        left, right, (((1,), (1,)), ((), ())), preferred_element_type=jnp.float32
    )


def on_device(
    inputs,
    conditioning,
    grid_sizes,
    ada_weight,
    ada_bias,
    qkv_weight,
    qv_bias,
    proj_weight,
    proj_bias,
    fc1_weight,
    fc1_bias,
    fc2_weight,
    fc2_bias,
    cotangent,
):
    images, strip_rows, model_width = inputs.shape
    head_size = model_width // HEADS
    row_count = images * strip_rows
    blocks = lax.axis_size("blk")
    data_count = lax.axis_size("dp")
    ada_full, qkv_full, proj_full, fc1_full, fc2_full = (
        lax.all_gather(ada_weight, "blk", axis=0, tiled=True),
        lax.all_gather(qkv_weight, "blk", axis=0, tiled=True),
        lax.all_gather(proj_weight, "blk", axis=0, tiled=True),
        lax.all_gather(fc1_weight, "blk", axis=0, tiled=True),
        lax.all_gather(fc2_weight, "blk", axis=0, tiled=True),
    )
    grid_areas = grid_sizes[:, 0] * grid_sizes[:, 1]
    positions = lax.axis_index("blk") * strip_rows + jnp.arange(strip_rows, dtype=jnp.int32)
    row_valid = (positions[None, :] < grid_areas[:, None])[:, :, None]
    cond_f32 = conditioning.astype(jnp.float32)
    silu_cond, silu_back = jax.vjp(jax.nn.silu, cond_f32)
    silu_low = silu_cond.astype(jnp.bfloat16)
    modulation = jnp.dot(silu_low, ada_full, preferred_element_type=jnp.float32) + ada_bias.astype(
        jnp.float32
    )
    pieces = [
        modulation[:, None, portion * model_width : (portion + 1) * model_width]
        for portion in range(6)
    ]
    shift_attn, scale_attn, gate_attn, shift_mlp, scale_mlp, gate_mlp = pieces
    inputs_f32 = inputs.astype(jnp.float32)
    normed_attn, norm_back_attn = jax.vjp(normalize, inputs_f32)
    h_attn = (
        (normed_attn * (1.0 + scale_attn) + shift_attn)
        .astype(jnp.bfloat16)
        .reshape(row_count, model_width)
    )
    qkv_rows = jnp.dot(h_attn, qkv_full, preferred_element_type=jnp.float32)
    bias_f32 = qv_bias.astype(jnp.float32)
    query_low = (qkv_rows[:, :model_width] + bias_f32[:model_width]).astype(jnp.bfloat16)
    key_low = qkv_rows[:, model_width : 2 * model_width].astype(jnp.bfloat16)
    value_low = (qkv_rows[:, 2 * model_width :] + bias_f32[model_width:]).astype(jnp.bfloat16)
    keys_all, values_all = (
        lax.all_gather(key_low.reshape(images, strip_rows, model_width), "blk", axis=1, tiled=True),
        lax.all_gather(
            value_low.reshape(images, strip_rows, model_width), "blk", axis=1, tiled=True
        ),
    )
    slot_total = keys_all.shape[1]
    query_heads = query_low.reshape(images, strip_rows, HEADS, head_size)
    key_heads = keys_all.reshape(images, slot_total, HEADS, head_size)
    value_heads = values_all.reshape(images, slot_total, HEADS, head_size)
    score_scale = head_size ** (-0.5)
    key_valid = (jnp.arange(slot_total, dtype=jnp.int32)[None, :] < grid_areas[:, None])[
        :, None, None, :
    ]

    def masked_scores():
        plain_scores = (
            jnp.einsum(
                "gqhd,gkhd->ghqk", query_heads, key_heads, preferred_element_type=jnp.float32
            )
            * score_scale
        )
        return jnp.where(key_valid, plain_scores, MASKED)

    scores = masked_scores()
    largest = jnp.max(scores, -1, keepdims=True)
    exponent = jnp.exp(scores - largest)
    totals = jnp.sum(exponent, -1, keepdims=True)
    log_total = largest + jnp.log(totals)
    probs_low = (exponent / totals).astype(jnp.bfloat16)
    attended = jnp.einsum(
        "ghqk,gkhd->gqhd", probs_low, value_heads, preferred_element_type=jnp.float32
    )
    attended_low = attended.reshape(row_count, model_width).astype(jnp.bfloat16)
    attn_out = (
        jnp.dot(attended_low, proj_full, preferred_element_type=jnp.float32)
        + proj_bias.astype(jnp.float32)
    ).reshape(images, strip_rows, model_width)
    middle = inputs_f32 + gate_attn * attn_out
    normed_mlp, norm_back_mlp = jax.vjp(normalize, middle)
    h_mlp = (
        (normed_mlp * (1.0 + scale_mlp) + shift_mlp)
        .astype(jnp.bfloat16)
        .reshape(row_count, model_width)
    )
    hidden_pre = jnp.dot(h_mlp, fc1_full, preferred_element_type=jnp.float32) + fc1_bias.astype(
        jnp.float32
    )
    activated, gelu_back = jax.vjp(gelu_tanh, hidden_pre)
    activated_low = activated.astype(jnp.bfloat16)
    mlp_out = (
        jnp.dot(activated_low, fc2_full, preferred_element_type=jnp.float32)
        + fc2_bias.astype(jnp.float32)
    ).reshape(images, strip_rows, model_width)
    result = middle + gate_mlp * mlp_out
    output = jnp.where(row_valid, result, 0.0).astype(jnp.bfloat16)
    grad_out = jnp.where(row_valid, cotangent.astype(jnp.float32), 0.0)
    grad_mlp = (gate_mlp * grad_out).astype(jnp.bfloat16).reshape(row_count, model_width)
    grad_gate_mlp = jnp.sum(grad_out * mlp_out, 1)
    fc2_term = transpose_product(activated_low, grad_mlp)
    fc2_bias_term = jnp.sum(grad_mlp.astype(jnp.float32), 0)
    grad_act = product_back(grad_mlp, fc2_full)
    grad_pre = gelu_back(grad_act)[0].astype(jnp.bfloat16)
    fc1_term = transpose_product(h_mlp, grad_pre)
    fc1_bias_term = jnp.sum(grad_pre.astype(jnp.float32), 0)
    grad_h_mlp = product_back(grad_pre, fc1_full).reshape(images, strip_rows, model_width)
    grad_shift_mlp = jnp.sum(grad_h_mlp, 1)
    grad_scale_mlp = jnp.sum(grad_h_mlp * normed_mlp, 1)
    grad_middle = grad_out + norm_back_mlp(grad_h_mlp * (1.0 + scale_mlp))[0]
    grad_attn = (gate_attn * grad_middle).astype(jnp.bfloat16).reshape(row_count, model_width)
    grad_gate_attn = jnp.sum(grad_middle * attn_out, 1)
    proj_term = transpose_product(attended_low, grad_attn)
    proj_bias_term = jnp.sum(grad_attn.astype(jnp.float32), 0)
    grad_attended = product_back(grad_attn, proj_full).astype(jnp.bfloat16)
    grad_heads = grad_attended.reshape(images, strip_rows, HEADS, head_size)
    probs_again = jnp.exp(masked_scores() - log_total)
    grad_probs = jnp.einsum(
        "gqhd,gkhd->ghqk", grad_heads, value_heads, preferred_element_type=jnp.float32
    )
    inner_sum = jnp.sum(probs_again * grad_probs, -1, keepdims=True)
    grad_scores = (probs_again * (grad_probs - inner_sum)).astype(jnp.bfloat16)
    grad_query = (
        jnp.einsum("ghqk,gkhd->gqhd", grad_scores, key_heads, preferred_element_type=jnp.float32)
        * score_scale
    )
    grad_keys_all = (
        jnp.einsum("ghqk,gqhd->gkhd", grad_scores, query_heads, preferred_element_type=jnp.float32)
        * score_scale
    )
    grad_values_all = jnp.einsum(
        "ghqk,gqhd->gkhd", probs_low, grad_heads, preferred_element_type=jnp.float32
    )
    grad_key, grad_value = (
        lax.psum_scatter(
            grad_keys_all.reshape(images, slot_total, model_width).astype(jnp.bfloat16),
            "blk",
            scatter_dimension=1,
            tiled=True,
        ).astype(jnp.float32),
        lax.psum_scatter(
            grad_values_all.reshape(images, slot_total, model_width).astype(jnp.bfloat16),
            "blk",
            scatter_dimension=1,
            tiled=True,
        ).astype(jnp.float32),
    )
    grad_query_low = grad_query.reshape(row_count, model_width).astype(jnp.bfloat16)
    grad_value_low = grad_value.reshape(row_count, model_width).astype(jnp.bfloat16)
    grad_qkv = jnp.concatenate(
        [
            grad_query_low,
            grad_key.reshape(row_count, model_width).astype(jnp.bfloat16),
            grad_value_low,
        ],
        1,
    )
    qkv_term = transpose_product(h_attn, grad_qkv)
    qv_bias_term = jnp.concatenate(
        [
            jnp.sum(grad_query_low.astype(jnp.float32), 0),
            jnp.sum(grad_value_low.astype(jnp.float32), 0),
        ]
    )
    grad_h_attn = product_back(grad_qkv, qkv_full).reshape(images, strip_rows, model_width)
    grad_shift_attn = jnp.sum(grad_h_attn, 1)
    grad_scale_attn = jnp.sum(grad_h_attn * normed_attn, 1)
    input_grad = grad_middle + norm_back_attn(grad_h_attn * (1.0 + scale_attn))[0]
    modulation_term = jnp.concatenate(
        [
            grad_shift_attn,
            grad_scale_attn,
            grad_gate_attn,
            grad_shift_mlp,
            grad_scale_mlp,
            grad_gate_mlp,
        ],
        1,
    )
    grad_modulation, qv_bias_sum, proj_bias_sum, fc1_bias_sum, fc2_bias_sum = (
        lax.psum(modulation_term.astype(jnp.bfloat16), "blk").astype(jnp.float32),
        lax.psum(qv_bias_term.astype(jnp.bfloat16), "blk").astype(jnp.float32),
        lax.psum(proj_bias_term.astype(jnp.bfloat16), "blk").astype(jnp.float32),
        lax.psum(fc1_bias_term.astype(jnp.bfloat16), "blk").astype(jnp.float32),
        lax.psum(fc2_bias_term.astype(jnp.bfloat16), "blk").astype(jnp.float32),
    )
    modulation_low = grad_modulation.astype(jnp.bfloat16)
    ada_term = transpose_product(silu_low, modulation_low) * (1.0 / blocks)
    ada_bias_term = jnp.sum(modulation_low.astype(jnp.float32), 0)
    cond_grad = silu_back(product_back(modulation_low, ada_full))[0]
    ada_bias_rows = ada_bias_term.reshape(data_count, -1)
    qv_bias_rows = qv_bias_sum.reshape(data_count, -1)
    proj_bias_rows = proj_bias_sum.reshape(data_count, -1)
    fc1_bias_rows = fc1_bias_sum.reshape(data_count, -1)
    fc2_bias_rows = fc2_bias_sum.reshape(data_count, -1)
    summed = (
        lax.psum_scatter(ada_term, "dp", scatter_dimension=0, tiled=True),
        lax.psum_scatter(qkv_term, "dp", scatter_dimension=0, tiled=True),
        lax.psum_scatter(proj_term, "dp", scatter_dimension=0, tiled=True),
        lax.psum_scatter(fc1_term, "dp", scatter_dimension=0, tiled=True),
        lax.psum_scatter(fc2_term, "dp", scatter_dimension=0, tiled=True),
        lax.psum_scatter(ada_bias_rows, "dp", scatter_dimension=0, tiled=True),
        lax.psum_scatter(qv_bias_rows, "dp", scatter_dimension=0, tiled=True),
        lax.psum_scatter(proj_bias_rows, "dp", scatter_dimension=0, tiled=True),
        lax.psum_scatter(fc1_bias_rows, "dp", scatter_dimension=0, tiled=True),
        lax.psum_scatter(fc2_bias_rows, "dp", scatter_dimension=0, tiled=True),
    )
    weight_sums = (
        lax.psum_scatter(
            summed[0].astype(jnp.bfloat16), "blk", scatter_dimension=1, tiled=True
        ).astype(jnp.float32),
        lax.psum_scatter(
            summed[1].astype(jnp.bfloat16), "blk", scatter_dimension=1, tiled=True
        ).astype(jnp.float32),
        lax.psum_scatter(
            summed[2].astype(jnp.bfloat16), "blk", scatter_dimension=1, tiled=True
        ).astype(jnp.float32),
        lax.psum_scatter(
            summed[3].astype(jnp.bfloat16), "blk", scatter_dimension=1, tiled=True
        ).astype(jnp.float32),
        lax.psum_scatter(
            summed[4].astype(jnp.bfloat16), "blk", scatter_dimension=1, tiled=True
        ).astype(jnp.float32),
    )
    bias_sums = summed[5:]
    return (
        output,
        input_grad,
        cond_grad,
        weight_sums[0],
        bias_sums[0].reshape(-1),
        weight_sums[1],
        bias_sums[1].reshape(-1),
        weight_sums[2],
        bias_sums[2].reshape(-1),
        weight_sums[3],
        bias_sums[3].reshape(-1),
        weight_sums[4],
        bias_sums[4].reshape(-1),
    )


def solution(mesh):
    placed = (
        P("dp", "blk", None),
        P("dp", None),
        P("dp", None),
        P("blk", None),
        P(),
        P("blk", None),
        P(),
        P("blk", None),
        P(),
        P("blk", None),
        P(),
        P("blk", None),
        P(),
        P("dp", "blk", None),
    )
    return jax.shard_map(
        on_device,
        mesh=mesh,
        in_specs=placed,
        out_specs=(
            P("dp", "blk", None),
            P("dp", "blk", None),
            P("dp", None),
            P("dp", "blk"),
            P("dp"),
            P("dp", "blk"),
            P("dp"),
            P("dp", "blk"),
            P("dp"),
            P("dp", "blk"),
            P("dp"),
            P("dp", "blk"),
            P("dp"),
        ),
        check_vma=False,
    )
```

profile of v0, /device:TPU:0, one launch (start us, length us, event | category | flops | bytes accessed | tf_op | source)
XLA Modules:
  0.0 1863.8 jit_solution(13993991798059226001)
XLA Ops:
  10.2 30.9 %all-gather.8.cloned.1.call-done = bf16[1152,6912]{1,0:T(8,128)(2,1)} async-done(((bf16[576,6912]{1,0:T(8,128)(2,1)}), bf16[1152,6912]{1,0:T(8,128)(2,1)}) %all-gather.8.cloned.1.call-update) | async-done | bytes 15925264 | tf_op jit(solution)/shard_map/all_gather | solution.py:57
  41.1 7.7 convolution_add_fusion
  50.4 12.8 all-gather.10.cloned.1.call-done
  63.1 5.8 fusion.58
  69.0 1.9 copy-done.20
  71.8 3.0 fusion.22
  79.0 1.8 reshape.292
  80.8 1.5 copy.64
  83.3 5.6 all-gather.20.cloned.1.call-done
  88.9 12.3 fusion.59
  101.3 1.6 copy.63
  102.9 10.8 all-gather.12.cloned.1.call-done
  113.7 1.6 copy.61
  115.3 2.0 fusion.8
  117.3 1.5 fusion.7
  119.4 1.4 divide_convert_fusion
  120.8 1.3 copy-done.3
  123.6 4.1 all-gather.16.cloned.1.call-done
  127.7 2.8 convolution_add_fusion.2
  133.3 20.1 %all-gather.18.cloned.1.call-done = bf16[1152,4608]{1,0:T(8,128)(2,1)} async-done(((bf16[576,4608]{1,0:T(8,128)(2,1)}), bf16[1152,4608]{1,0:T(8,128)(2,1)}) %all-gather.18.cloned.1.call-update) | async-done | bytes 10616848 | tf_op jit(solution)/shard_map/all_gather | solution.py:60
  153.5 10.0 fusion.51
  163.5 8.8 fusion.60
  173.5 7.7 convolution_add_fusion.3
  181.1 1.3 add_add_fusion.1
  183.3 2.0 fusion.53
  186.1 3.6 convolution_convert_fusion
  189.8 3.8 reshape.293
  193.6 2.6 copy.67
  196.2 2.6 convolution_convert_fusion.1
  198.8 2.5 copy.72
  201.4 3.6 multiply_reduce_fusion
  205.1 1.3 multiply_convert_fusion.1
  206.4 1.5 multiply_convert_fusion.2
  207.9 2.5 copy.70
  210.5 4.3 fusion.27
  215.1 2.2 fusion.57
  218.1 1.5 copy.74
  219.6 3.9 reduce-scatter.25.cloned.1.call-done
  223.5 1.3 copy.73
  224.9 7.8 fusion.25
  233.7 13.6 fusion.49
  247.4 1.6 copy-done.22
  249.1 8.9 fusion.61
  259.7 6.0 fusion.26
  267.9 1.9 multiply_reduce_fusion.1
  269.9 3.9 all-reduce.8
  273.8 12.9 convolution_multiply_fusion
  286.8 83.9 %reduce-scatter.47.cloned.1.call-done = f32[72,1152]{1,0:T(8,128)} async-done(((f32[1152,1152]{1,0:T(8,128)}), f32[72,1152]{1,0:T(8,128)}) %reduce-scatter.47.cloned.1.call-update) | async-done | bytes 331792
  372.7 254.9 %reduce-scatter.45.cloned.1.call-done = f32[72,3456]{1,0:T(8,128)} async-done(((f32[1152,3456]{1,0:T(8,128)}), f32[72,3456]{1,0:T(8,128)}) %reduce-scatter.45.cloned.1.call-update) | async-done | bytes 995344
  627.7 1.3 convert_element_type.209
  630.2 316.5 %reduce-scatter.35.cloned.1.call-done = f32[288,1152]{1,0:T(8,128)} async-done(((f32[4608,1152]{1,0:T(8,128)}), f32[288,1152]{1,0:T(8,128)}) %reduce-scatter.35.cloned.1.call-update) | async-done | bytes 1327120 | tf_op jit(solution)/shard_map/reduce_scatter | solution.py:248
  946.7 1.4 convert_element_type.217
  948.1 1.3 copy.81
  949.5 316.9 %reduce-scatter.31.cloned.1.call-done = f32[72,4608]{1,0:T(8,128)} async-done(((f32[1152,4608]{1,0:T(8,128)}), f32[72,4608]{1,0:T(8,128)}) %reduce-scatter.31.cloned.1.call-update) | async-done | bytes 1327120 | tf_op jit(solution)/shard_map/reduce_scatter | solution.py:247
  1266.4 2.2 convert_element_type.215
  1268.7 481.8 %reduce-scatter.29.cloned.1.call-done = f32[72,6912]{1,0:T(8,128)} async-done(((f32[1152,6912]{1,0:T(8,128)}), f32[72,6912]{1,0:T(8,128)}) %reduce-scatter.29.cloned.1.call-update) | async-done | bytes 1990672 | tf_op jit(solution)/shard_map/reduce_scatter | solution.py:244
  1750.5 1.7 convert_element_type.206
  1752.2 1.7 copy.75
  1754.6 76.7 %all-reduce.7 = (f32[16,432]{1,0:T(8,128)S(1)}, f32[16,144]{1,0:T(8,128)S(1)}, f32[16,72]{1,0:T(8,128)S(1)}, f32[16,288]{1,0:T(8,128)S(1)}, f32[16,72]{1,0:T(8,128)S(1)}) all-reduce(f32[16,432]{1,0:T(8,128)S(1)} %reshape.263, bf16[16,144]{1,0:T(8,128)(2,1)S(1)} %get-tuple-element.27, ...), channel_id=6, replica_groups=mesh['dp'=16,'blk'=2] {'dp'}, use_global_device_ids=true, to_apply=%region_23.24.clone | all-reduce | flops 16128 | bytes 110592
  1831.3 1.2 dynamic-slice_reduce_fusion
  1835.0 1.2 constant_dynamic-slice_fusion.3
  1836.2 10.4 fusion.38
  1852.4 1.9 convert_element_type.216
  1854.3 1.5 copy.76
  (265 shorter events, 37.7 us)
Async XLA Ops:
  7.2 33.9 %all-gather.8.cloned.1.call-start = ((), (), s32[]{:S(2)}) async-start(), calls=%async_computation.12 | async-start | bytes 23887872 | tf_op jit(solution)/shard_map/all_gather | solution.py:57
  7.9 55.2 %all-gather.10.cloned.1.call-start = ((), (), s32[]{:S(2)}) async-start(), calls=%async_computation.13 | async-start | bytes 11943936 | tf_op jit(solution)/shard_map/all_gather | solution.py:58
  8.7 32.4 %copy-start.45 = (bf16[2,1152]{1,0:T(2,128)(2,1)S(1)}, bf16[2,1152]{1,0:T(2,128)(2,1)}, u32[]{:S(2)}) copy-start(bf16[2,1152]{1,0:T(2,128)(2,1)} %param.15) | copy-start | bytes 13828
  8.7 80.2 %all-gather.20.cloned.1.call-start = ((), (), s32[]{:S(2)}) async-start(), calls=%async_computation.18 | async-start | bytes 15925248 | tf_op jit(solution)/shard_map/all_gather | solution.py:61
  9.4 91.9 %all-gather.14.cloned.1.call-start = ((), (), s32[]{:S(2)}) async-start(), calls=%async_computation.15 | async-start | bytes 1769472 | tf_op jit(solution)/shard_map/all_gather | solution.py:90
  9.9 39.5 %copy-start.48 = (f32[2,128]{1,0:T(2,128)}, f32[2,128]{1,0:T(2,128)S(1)}, u32[]{:S(2)}) copy-start(f32[2,128]{1,0:T(2,128)S(1)} %broadcast_multiply_fusion.1) | copy-start | bytes 3076
  10.2 30.9 %copy-start.68 = (f32[2,128]{1,0:T(2,128)}, f32[2,128]{1,0:T(2,128)S(1)}, u32[]{:S(2)}) copy-start(f32[2,128]{1,0:T(2,128)S(1)} %fusion.20) | copy-start | bytes 3076
  10.2 39.2 %copy-start.57 = (f32[2,128]{1,0:T(2,128)}, f32[2,128]{1,0:T(2,128)S(1)}, u32[]{:S(2)}) copy-start(f32[2,128]{1,0:T(2,128)S(1)} %fusion.39) | copy-start | bytes 3076
  49.4 32.9 %copy-start.43 = (f32[2,1152]{1,0:T(2,128)}, f32[2,1152]{1,0:T(2,128)S(1)}, u32[]{:S(2)}) copy-start(f32[2,1152]{1,0:T(2,128)S(1)} %get-tuple-element.44) | copy-start | bytes 27652
  50.4 18.6 copy-start.26
  63.1 8.6 copy-start.47
  71.7 42.0 %all-gather.12.cloned.1.call-start = ((), (), s32[]{:S(2)}) async-start(), calls=%async_computation.14 | async-start | bytes 1769472 | tf_op jit(solution)/shard_map/all_gather | solution.py:91
  74.8 52.9 %all-gather.16.cloned.1.call-start = ((), (), s32[]{:S(2)}) async-start(), calls=%async_computation.16 | async-start | bytes 3981312 | tf_op jit(solution)/shard_map/all_gather | solution.py:59
  75.4 2.1 copy-start.65
  75.5 2.7 copy-start.78
  75.5 78.0 %all-gather.18.cloned.1.call-start = ((), (), s32[]{:S(2)}) async-start(), calls=%async_computation.17 | async-start | bytes 15925248 | tf_op jit(solution)/shard_map/all_gather | solution.py:60
  76.2 6.2 copy-start.10
  76.2 141.9 %reduce-scatter.27.cloned.1.call-start = ((), (), s32[]{:S(2)}) async-start(), calls=%async_computation.20 | async-start | bytes 1769472 | tf_op jit(solution)/shard_map/reduce_scatter | solution.py:188
  79.0 4.2 copy-start.73
  83.3 18.0 copy-start.24
  102.9 14.4 copy-start.7
  115.3 5.6 copy-start.8
  117.3 2.1 copy-start
  123.6 6.9 copy-start.18
  127.7 2.8 copy-start.42
  130.5 2.8 copy-start.14
  163.4 8.8 copy-start.21
  163.4 10.0 copy-start.13
  163.5 8.8 copy-start.41
  163.5 8.8 copy-start.52
  163.5 8.8 copy-start.62
  173.4 7.7 copy-start.44
  173.4 7.7 copy-start.74
  182.5 2.9 copy-start.5
  189.8 6.4 copy-start.4
  198.8 2.6 copy-start.39
  198.8 2.6 copy-start.9
  198.8 2.6 copy-start.12
  198.8 2.6 copy-start.54
  201.3 22.2 %reduce-scatter.25.cloned.1.call-start = ((), (), s32[]{:S(2)}) async-start(), calls=%async_computation.19 | async-start | bytes 1769472 | tf_op jit(solution)/shard_map/reduce_scatter | solution.py:182
  201.4 3.6 copy-start.1
  207.9 2.6 copy-start.19
  210.4 160.3 %reduce-scatter.47.cloned.1.call-start = ((), (), s32[]{:S(2)}) async-start(), calls=%async_computation.30 | async-start | bytes 5640192
  214.9 412.8 %reduce-scatter.45.cloned.1.call-start = ((), (), s32[]{:S(2)}) async-start(), calls=%async_computation.29 | async-start | bytes 16920576
  217.4 7.5 copy-start.27
  218.1 14.6 copy-start.28
  219.6 13.0 copy-start.30
  224.8 7.8 copy-start.32
  232.7 714.0 %reduce-scatter.35.cloned.1.call-start = ((), (), s32[]{:S(2)}) async-start(), calls=%async_computation.24 | async-start | bytes 22560768 | tf_op jit(solution)/shard_map/reduce_scatter | solution.py:248
  247.4 1019.0 %reduce-scatter.31.cloned.1.call-start = ((), (), s32[]{:S(2)}) async-start(), calls=%async_computation.22 | async-start | bytes 22560768 | tf_op jit(solution)/shard_map/reduce_scatter | solution.py:247
  258.1 1492.4 %reduce-scatter.29.cloned.1.call-start = ((), (), s32[]{:S(2)}) async-start(), calls=%async_computation.21 | async-start | bytes 33841152 | tf_op jit(solution)/shard_map/reduce_scatter | solution.py:244
  259.7 6.0 copy-start.37
  259.7 6.0 copy-start.49
  259.7 6.4 copy-start.69
  259.7 6.4 copy-start.58
  265.7 2.2 copy-start.17
  265.8 2.1 copy-start.67
  265.8 2.1 copy-start.75
  267.9 5.9 copy-start.46
  286.8 1559.8 %reduce-scatter.41.cloned.1.call-start = ((), (), s32[]{:S(2)}) async-start(), calls=%async_computation.27 | async-start | bytes 442368
  372.7 1475.6 %reduce-scatter.39.cloned.1.call-start = ((), (), s32[]{:S(2)}) async-start(), calls=%async_computation.26 | async-start | bytes 1327104
  630.2 1220.1 %reduce-scatter.43.cloned.1.call-start = ((), (), s32[]{:S(2)}) async-start(), calls=%async_computation.28 | async-start | bytes 1327104
  949.4 903.0 %reduce-scatter.33.cloned.1.call-start = ((), (), s32[]{:S(2)}) async-start(), calls=%async_computation.23 | async-start | bytes 995328 | tf_op jit(solution)/shard_map/reduce_scatter | solution.py:265
  1268.6 585.7 %reduce-scatter.37.cloned.1.call-start = ((), (), s32[]{:S(2)}) async-start(), calls=%async_computation.25 | async-start | bytes 2654208
  (35 other events, 44.4 us)
Sparse Core Ops, SparseCore 0:
  9.6 31.5 all-gather.7
  42.7 20.4 all-gather.9
  64.7 24.1 all-gather.19
  90.9 10.3 all-gather.13
  103.3 10.3 all-gather.11
  115.1 12.5 all-gather.15
  129.3 24.1 all-gather.17
  201.4 9.8 reduce-scatter.26
  213.6 9.8 reduce-scatter.24
  228.6 142.0 reduce-scatter.46
  376.6 251.0 reduce-scatter.44
  633.5 313.1 reduce-scatter.34
  953.7 312.6 reduce-scatter.30
  1272.3 478.1 reduce-scatter.28
  1753.2 7.3 reduce-scatter.40
  1763.3 9.4 reduce-scatter.38
  1775.0 9.4 reduce-scatter.42
  1787.2 9.2 reduce-scatter.32
  1798.9 10.4 reduce-scatter.36
where the time goes:
time: 1870 us; the launch traced here: 1860 us
  waiting for transfers between devices  1550 us (83%)
  matrix products  135 us (7%)
  blocking collectives  80.6 us (4%)
  local copies, waits for them, and re-layouts  50.8 us (3%)
  other arithmetic  34.4 us (2%)
    reduce_scatter x1, waiting for transfers between devices, on_device(): lax.psum_scatter(ada_term, 'dp', scatter_dimension=0, tiled=True)  482 us
    unnamed x25, waiting for transfers between devices  342 us
    reduce_scatter x1, waiting for transfers between devices, on_device(): lax.psum_scatter(fc1_term, 'dp', scatter_dimension=0, tiled=True)  317 us
    reduce_scatter x1, waiting for transfers between devices, on_device(): lax.psum_scatter(fc2_term, 'dp', scatter_dimension=0, tiled=True)  316 us
    unnamed x1, blocking collectives  76.7 us
    dot_general x5, matrix products, transpose_product(): lax.dot_general(left, right, (((0,), (0,)), ((), ())), preferred_element_...  47.6 us
    dot_general x5, matrix products, product_back(): lax.dot_general(left, right, (((1,), (1,)), ((), ())), preferred_element_...  41 us
  transfers between devices with their start and end apart: 19, of which 13 were waited for; matrix products, arithmetic and copies ran while one was open for 9% of the time, Pallas kernels for 0%

commit v1 on v0

v1 whole, which is shorter than its diff:
```python
import functools

import jax
import jax.numpy as jnp
from jax import lax
from jax.experimental import pallas as pl
from jax.experimental.pallas import tpu as pltpu
from jax.sharding import PartitionSpec as P

HEADS = 16
EPS = 1e-06
MASKED = -1e30
F32 = jnp.float32
BF16 = jnp.bfloat16
VMEM_LIMIT = 48 * 1024 * 1024


def normalize(values_in):
    average = jnp.mean(values_in, -1, keepdims=True)
    centred = values_in - average
    return centred * lax.rsqrt(jnp.mean(centred * centred, -1, keepdims=True) + EPS)


def gelu_tanh(values_in):
    return jax.nn.gelu(values_in, approximate=True)


def product(left, right):
    return jnp.dot(left, right, preferred_element_type=F32)


def transpose_product(left, right):
    return lax.dot_general(left, right, (((0,), (0,)), ((), ())), preferred_element_type=F32)


def product_back(left, right):
    return lax.dot_general(left, right, (((1,), (1,)), ((), ())), preferred_element_type=F32)


def swap(values_in):
    return lax.ppermute(values_in, "blk", [(0, 1), (1, 0)])


def pick(values_in, index, axis=0):
    return lax.dynamic_index_in_dim(values_in, index, axis, keepdims=False)


def in_order(core, mine, theirs, axis=0):
    first = jnp.where(core == 0, mine, theirs)
    second = jnp.where(core == 0, theirs, mine)
    return jnp.concatenate([first, second], axis)


def head_window(head, size):
    low, high = head * size, (head + 1) * size
    start, stop = low // 128 * 128, -(-high // 128) * 128
    lane = lax.broadcasted_iota(jnp.int32, (1, stop - start), 1) + start
    return slice(start, stop), (lane >= low) & (lane < high)


def attention_forward_kernel(size, scale, q_ref, k_ref, v_ref, valid_ref, out_ref, log_ref):
    valid = valid_ref[...] > 0
    rows = q_ref.shape[0]
    lane = lax.broadcasted_iota(jnp.int32, (1, 128), 1)
    logs = jnp.zeros((rows, 128), F32)
    for head in range(HEADS):
        columns, own = head_window(head, size)
        query = jnp.where(own, q_ref[:, columns].astype(F32), 0.0).astype(BF16)
        scores = jnp.where(valid, product_back(query, k_ref[:, columns]) * scale, MASKED)
        largest = jnp.max(scores, -1, keepdims=True)
        exponent = jnp.exp(scores - largest)
        totals = jnp.sum(exponent, -1, keepdims=True)
        probs = (exponent / totals).astype(BF16)
        attended = product(probs, v_ref[:, columns])
        out_ref[:, columns] = jnp.where(own, attended, out_ref[:, columns].astype(F32)).astype(BF16)
        logs = jnp.where(lane == head, largest + jnp.log(totals), logs)
    log_ref[...] = logs


def attention_backward_kernel(
    size, scale, q_ref, k_ref, v_ref, valid_ref, log_ref, grad_ref, gq_ref, gk_ref, gv_ref
):
    valid = valid_ref[...] > 0
    for head in range(HEADS):
        columns, own = head_window(head, size)
        query = q_ref[:, columns]
        key = k_ref[:, columns]
        grad = grad_ref[:, columns]
        own_query = jnp.where(own, query.astype(F32), 0.0).astype(BF16)
        own_grad = jnp.where(own, grad.astype(F32), 0.0).astype(BF16)
        scores = jnp.where(valid, product_back(own_query, key) * scale, MASKED)
        probs = jnp.exp(scores - log_ref[:, head : head + 1])
        grad_probs = product_back(own_grad, v_ref[:, columns])
        inner = jnp.sum(probs * grad_probs, -1, keepdims=True)
        grad_scores = (probs * (grad_probs - inner)).astype(BF16)
        grad_query = product(grad_scores, key) * scale
        grad_key = transpose_product(grad_scores, query) * scale
        grad_value = transpose_product(probs.astype(BF16), grad)
        gq_ref[:, columns] = jnp.where(own, grad_query, gq_ref[:, columns].astype(F32)).astype(BF16)
        gk_ref[:, columns] = jnp.where(own, grad_key, gk_ref[:, columns].astype(F32)).astype(BF16)
        gv_ref[:, columns] = jnp.where(own, grad_value, gv_ref[:, columns].astype(F32)).astype(BF16)


def attention_forward(query, key, value, valid):
    rows, width = query.shape
    size = width // HEADS
    return pl.pallas_call(
        functools.partial(attention_forward_kernel, size, size ** (-0.5)),
        out_shape=(
            jax.ShapeDtypeStruct((rows, width), BF16),
            jax.ShapeDtypeStruct((rows, 128), F32),
        ),
        compiler_params=pltpu.CompilerParams(vmem_limit_bytes=VMEM_LIMIT),
        cost_estimate=pl.CostEstimate(
            flops=8 * rows * rows * 256 * HEADS, bytes_accessed=8 * rows * width, transcendentals=rows * rows * HEADS
        ),
        name="attention_forward",
    )(query, key, value, valid)


def attention_backward(query, key, value, valid, logs, grad):
    rows, width = query.shape
    size = width // HEADS
    shape = jax.ShapeDtypeStruct((rows, width), BF16)
    return pl.pallas_call(
        functools.partial(attention_backward_kernel, size, size ** (-0.5)),
        out_shape=(shape, shape, shape),
        compiler_params=pltpu.CompilerParams(vmem_limit_bytes=VMEM_LIMIT),
        cost_estimate=pl.CostEstimate(
            flops=20 * rows * rows * 256 * HEADS, bytes_accessed=14 * rows * width, transcendentals=rows * rows * HEADS
        ),
        name="attention_backward",
    )(query, key, value, valid, logs, grad)


def axis_orders(count):
    bits = count.bit_length() - 1
    if bits == 4:
        return [(0, 1, 2, 3), (1, 2, 0, 3), (2, 0, 1, 3)]
    return [tuple((bit + turn) % bits for bit in range(bits)) for turn in range(min(3, bits))]


def reduce_chunk(values_in, order, count):
    bits = count.bit_length() - 1
    place = lax.axis_index("dp")
    left = list(range(bits - 1, -1, -1))
    current = values_in.reshape((2,) * bits + values_in.shape[1:])
    for step, bit in enumerate(order):
        mine = (place >> bit) & 1
        axis = left.index(bit)
        send = pick(current, 1 - mine, axis).astype(BF16)
        keep = pick(current, mine, axis)
        left.pop(axis)
        got = lax.ppermute(send, "dp", [(index, index ^ (1 << bit)) for index in range(count)])
        current = keep.astype(F32) + got.astype(F32)
        if step < bits - 1:
            current = current.astype(BF16)
    return current


def cut(rows):
    if rows % 8 or rows < 24:
        return [rows]
    tiles = rows // 8
    first = round(tiles * 4 / 9)
    second = round(tiles * 3 / 9)
    return [8 * first, 8 * second, rows - 8 * first - 8 * second]


def reduce_scatter(values_in):
    count = lax.axis_size("dp")
    rows = values_in.shape[0] // count
    blocks = values_in.reshape(count, rows, values_in.shape[1])
    done, start = [], 0
    for length, order in zip(cut(rows), axis_orders(count)):
        done.append(reduce_chunk(blocks[:, start : start + length], order, count))
        start += length
    return jnp.concatenate(done, 0)


def small_reduce_scatter(rows_in):
    count = lax.axis_size("dp")
    bits = count.bit_length() - 1
    place = lax.axis_index("dp")
    current = rows_in.reshape((2,) * bits + rows_in.shape[1:])
    for bit in range(bits - 1, -1, -1):
        mine = (place >> bit) & 1
        send = pick(current, 1 - mine)
        keep = pick(current, mine)
        got = lax.ppermute(send, "dp", [(index, index ^ (1 << bit)) for index in range(count)])
        current = keep + got
    return current


def gather_unordered(values_in):
    count = lax.axis_size("dp")
    current = values_in
    for bit in range(count.bit_length() - 1):
        got = lax.ppermute(current, "dp", [(index, index ^ (1 << bit)) for index in range(count)])
        current = jnp.concatenate([current, got], 0)
    return current


def on_device(
    inputs,
    conditioning,
    grid_sizes,
    ada_weight,
    ada_bias,
    qkv_weight,
    qv_bias,
    proj_weight,
    proj_bias,
    fc1_weight,
    fc1_bias,
    fc2_weight,
    fc2_bias,
    cotangent,
):
    images, strip, width = inputs.shape
    data_count = lax.axis_size("dp")
    core = lax.axis_index("blk")
    other = 1 - core
    place = lax.axis_index("dp")
    part = ada_weight.shape[0]
    hidden = fc1_weight.shape[1]
    half_hidden = hidden // 2

    mine_inputs, their_inputs = pick(inputs, core), swap(pick(inputs, other))
    mine_cot, their_cot = pick(cotangent, core), swap(pick(cotangent, other))
    qkv_full = in_order(core, qkv_weight, swap(qkv_weight))
    proj_full = in_order(core, proj_weight, swap(proj_weight))
    fc1_parts = fc1_weight.reshape(part, 2, half_hidden)
    fc1_half = in_order(core, pick(fc1_parts, core, 1), swap(pick(fc1_parts, other, 1)))

    cond_f32 = conditioning.astype(F32)
    silu_cond, silu_back = jax.vjp(jax.nn.silu, cond_f32)
    silu_low = silu_cond.astype(BF16)
    modulation_part = product(pick(silu_low.reshape(images, 2, part), core, 1), ada_weight)
    modulation = modulation_part + swap(modulation_part) + ada_bias.astype(F32)
    own_modulation = pick(modulation, core)[None, :]
    shift_attn, scale_attn, gate_attn, shift_mlp, scale_mlp, gate_mlp = [
        own_modulation[:, index * width : (index + 1) * width] for index in range(6)
    ]
    silu_all = gather_unordered(silu_low)
    silu_rows = pick(silu_all.reshape(images * data_count, data_count, width // data_count), place, 1)

    area = pick(grid_sizes[:, 0] * grid_sizes[:, 1], core)
    near = jnp.arange(strip, dtype=jnp.int32)
    positions = jnp.concatenate([core * strip + near, other * strip + near])
    valid = positions < area
    valid_row = valid.astype(F32)[None, :]
    valid_column = valid[:, None]

    tokens = jnp.concatenate([mine_inputs, their_inputs], 0).astype(F32)
    cot = jnp.concatenate([mine_cot, their_cot], 0).astype(F32)
    grad_out = jnp.where(valid_column, cot, 0.0)
    grad_mlp = (gate_mlp * grad_out).astype(BF16)
    grad_mlp_other = swap(grad_mlp)
    grad_mlp_all = jnp.concatenate([grad_mlp, grad_mlp_other], 0)

    normed_attn, norm_back_attn = jax.vjp(normalize, tokens)
    h_attn = (normed_attn * (1.0 + scale_attn) + shift_attn).astype(BF16)
    h_attn_all = jnp.concatenate([h_attn, swap(h_attn)], 0)
    qkv_rows = product(h_attn, qkv_full)
    bias_f32 = qv_bias.astype(F32)
    query = (qkv_rows[:, :width] + bias_f32[:width]).astype(BF16)
    key = qkv_rows[:, width : 2 * width].astype(BF16)
    value = (qkv_rows[:, 2 * width :] + bias_f32[width:]).astype(BF16)
    attended, logs = attention_forward(query, key, value, valid_row)
    attended_all = jnp.concatenate([attended, swap(attended)], 0)
    attn = product(attended, proj_full) + proj_bias.astype(F32)
    middle = tokens + gate_attn * attn
    normed_mlp, norm_back_mlp = jax.vjp(normalize, middle)
    h_mlp = (normed_mlp * (1.0 + scale_mlp) + shift_mlp).astype(BF16)
    h_mlp_all = jnp.concatenate([h_mlp, swap(h_mlp)], 0)

    fc1_bias_half = pick(fc1_bias.astype(F32).reshape(2, half_hidden), core)
    hidden_pre = product(h_mlp_all, fc1_half) + fc1_bias_half
    activated, gelu_back = jax.vjp(gelu_tanh, hidden_pre)
    activated_low = activated.astype(BF16)
    grad_act = product_back(grad_mlp_all, fc2_weight)
    grad_pre = gelu_back(grad_act)[0].astype(BF16)
    fc1_term = transpose_product(h_mlp_all, grad_pre)
    fc1_grad = reduce_scatter(fc1_term)

    rows = images * strip
    grad_mlp_columns = pick(grad_mlp_all.reshape(2 * rows, 2, part), core, 1)
    grad_mlp_turned = jnp.concatenate([grad_mlp_columns[rows:], grad_mlp_columns[:rows]], 0)
    fc2_term = in_order(
        core,
        transpose_product(activated_low, grad_mlp_columns).astype(BF16),
        transpose_product(swap(activated_low), grad_mlp_turned).astype(BF16),
    )
    fc2_grad = reduce_scatter(fc2_term)

    mlp_part = product(activated_low, fc2_weight)
    mlp = mlp_part[:rows] + swap(mlp_part[rows:]) + fc2_bias.astype(F32)
    result = jnp.where(valid_column, middle + gate_mlp * mlp, 0.0).astype(BF16)
    grad_h_part = product_back(grad_pre, fc1_half)
    grad_h_mlp = grad_h_part[:rows] + swap(grad_h_part[rows:])

    grad_middle = grad_out + norm_back_mlp(grad_h_mlp * (1.0 + scale_mlp))[0]
    grad_attn = (gate_attn * grad_middle).astype(BF16)
    grad_attn_parts = grad_attn.reshape(rows, 2, part)
    grad_attn_columns = jnp.concatenate(
        [pick(grad_attn_parts, core, 1), swap(pick(grad_attn_parts, other, 1))], 0
    )
    proj_term = transpose_product(attended_all, grad_attn_columns)
    proj_grad = reduce_scatter(proj_term)
    grad_attended = product_back(grad_attn, proj_full).astype(BF16)
    grad_query, grad_key, grad_value = attention_backward(
        query, key, value, valid_row, logs, grad_attended
    )
    grad_qkv = jnp.concatenate([grad_query, grad_key, grad_value], 1)
    grad_qkv_parts = grad_qkv.reshape(rows, 2, 3 * part)
    grad_qkv_columns = jnp.concatenate(
        [pick(grad_qkv_parts, core, 1), swap(pick(grad_qkv_parts, other, 1))], 0
    )
    qkv_term = transpose_product(h_attn_all, grad_qkv_columns)
    qkv_grad = reduce_scatter(qkv_term)

    grad_h_attn = product_back(grad_qkv, qkv_full)
    input_grad = grad_middle + norm_back_attn(grad_h_attn * (1.0 + scale_attn))[0]

    grad_modulation = jnp.concatenate(
        [
            jnp.sum(grad_h_attn, 0),
            jnp.sum(grad_h_attn * normed_attn, 0),
            jnp.sum(grad_middle * attn, 0),
            jnp.sum(grad_h_mlp, 0),
            jnp.sum(grad_h_mlp * normed_mlp, 0),
            jnp.sum(grad_out * mlp, 0),
        ]
    ).astype(BF16)[None, :]
    modulation_low = in_order(core, grad_modulation, swap(grad_modulation))
    silu_grad_part = product_back(modulation_low, ada_weight)
    silu_grad = in_order(core, silu_grad_part, swap(silu_grad_part), 1)
    cond_grad = silu_back(silu_grad)[0]
    modulation_columns = pick(modulation_low.reshape(images, 2, 3 * width), core, 1)
    modulation_all = gather_unordered(modulation_columns)
    ada_grad = transpose_product(silu_rows, modulation_all)

    sum_f32 = lambda array: jnp.sum(array.astype(F32), 0)
    fc1_bias_part = sum_f32(grad_pre)
    fc1_bias_sums = in_order(core, fc1_bias_part, jnp.zeros_like(fc1_bias_part))
    bias_rows = jnp.concatenate(
        [
            sum_f32(grad_modulation).reshape(data_count, -1),
            jnp.concatenate([sum_f32(grad_query), sum_f32(grad_value)]).reshape(data_count, -1),
            sum_f32(grad_attn).reshape(data_count, -1),
            fc1_bias_sums.reshape(data_count, -1),
            sum_f32(grad_mlp).reshape(data_count, -1),
        ],
        1,
    )
    bias_sums = small_reduce_scatter(bias_rows + swap(bias_rows))
    lengths = [6 * width, 2 * width, width, hidden, width]
    ends, at = [], 0
    for length in lengths:
        at += length // data_count
        ends.append(at)
    biases = jnp.split(bias_sums, ends[:-1])

    back = lambda array: in_order(core, array[None, :strip], swap(array[None, strip:]))
    return (
        back(result),
        back(input_grad),
        cond_grad,
        ada_grad,
        biases[0],
        qkv_grad,
        biases[1],
        proj_grad,
        biases[2],
        fc1_grad,
        biases[3],
        fc2_grad,
        biases[4],
    )


def solution(mesh):
    rows = P("dp", "blk", None)
    weight = P("blk", None)
    grads = (P("dp", "blk"), P("dp"))
    placed = (rows, P("dp", None), P("dp", None)) + (weight, P()) * 5 + (rows,)
    return jax.shard_map(
        on_device,
        mesh=mesh,
        in_specs=placed,
        out_specs=(rows, rows, P("dp", None)) + grads * 5,
        check_vma=False,
    )
```

time: 1870 us -> 500 us (0.27)
  waiting for transfers between devices: 1550 us -> 177 us
  blocking collectives: 80.6 us -> 0 us
  matrix products: 135 us -> 61.3 us
  starting transfers between devices: 1.24 us -> 72.9 us
  local copies, waits for them, and re-layouts: 50.8 us -> 112 us
  other arithmetic: 34.4 us -> 57.3 us
    reduce_scatter x6 -> x0, waiting for transfers between devices: 1120 us -> none  [the longest x1 482 us: on_device(): lax.psum_scatter(ada_term, 'dp', scatter_dimension=0, tiled=True)]
    unnamed x25 -> x0, waiting for transfers between devices: 342 us -> none
    ppermute x0 -> x80, waiting for transfers between devices: none -> 177 us  [the longest x48 147 us: reduce_chunk(): lax.ppermute(send, 'dp', [(index, index ^ 1 << bit) for index in range(co...]
    all_gather x7 -> x0, waiting for transfers between devices: 84.4 us -> none  [the longest x1 30.9 us: on_device(): lax.all_gather(ada_weight, 'blk', axis=0, tiled=True)]
    unnamed x1 -> x0, blocking collectives: 76.7 us -> none
    ppermute x0 -> x80, starting transfers between devices: none -> 72.9 us  [the longest x48 49.8 us: reduce_chunk(): lax.ppermute(send, 'dp', [(index, index ^ 1 << bit) for index in range(co...]
    dot_general x5 -> x6, matrix products: 47.6 us -> 17.9 us  [transpose_product(): lax.dot_general(left, right, (((0,), (0,)), ((), ())), preferred_element_...]
    dot_general x11 -> x5, matrix products: 46.8 us -> 21 us  [product(): return jnp.dot(left, right, preferred_element_type=F32)]
  transfers between devices with their start and end apart: 19 -> 80, of which waited for: 13 -> 42; matrix products, arithmetic and copies ran while one was open for 9% -> 40% of each run, Pallas kernels for 0% -> 2%
where the time goes in v1:
time: 500 us; the launch traced here: 494 us
  waiting for transfers between devices  177 us (35%)
  local copies, waits for them, and re-layouts  112 us (22%)
  starting transfers between devices  72.9 us (15%)
  matrix products  61.3 us (12%)
  other arithmetic  57.3 us (11%)
  Pallas kernels  9.51 us (2%)
    ppermute x48, waiting for transfers between devices, reduce_chunk(): lax.ppermute(send, 'dp', [(index, index ^ 1 << bit) for index in range(co...  147 us
    ppermute x48, starting transfers between devices, reduce_chunk(): lax.ppermute(send, 'dp', [(index, index ^ 1 << bit) for index in range(co...  49.8 us
    dot_general x5, matrix products, product_back(): lax.dot_general(left, right, (((1,), (1,)), ((), ())), preferred_element_...  22.4 us
    dot_general x5, matrix products, product(): return jnp.dot(left, right, preferred_element_type=F32)  21 us
    dynamic_slice x12, local copies, waits for them, and re-layouts, pick(): return lax.dynamic_index_in_dim(values_in, index, axis, keepdims=False)  19.4 us
    convert_element_type x36, other arithmetic, reduce_chunk(): current = current.astype(BF16)  18.6 us
    dot_general x6, matrix products, transpose_product(): lax.dot_general(left, right, (((0,), (0,)), ((), ())), preferred_element_...  17.9 us
    ppermute x8, waiting for transfers between devices, gather_unordered(): lax.ppermute(current, 'dp', [(index, index ^ 1 << bit) for index in range...  17.6 us
  transfers between devices with their start and end apart: 80, of which 42 were waited for; matrix products, arithmetic and copies ran while one was open for 40% of the time, Pallas kernels for 2%

profile of v1, /device:TPU:0, one launch (start us, length us, event | category | flops | bytes accessed | tf_op | source)
XLA Modules:
  0.0 493.5 jit_solution(15991275779158041341)
XLA Ops:
  0.6 8.1 %reshape.404 = bf16[576,2,2304]{2,1,0:T(2,128)(2,1)} reshape(bf16[576,4608]{1,0:T(8,128)(2,1)} %param.23) | data formatting | bytes 10616832 | tf_op jit(solution)/shard_map/reshape | solution.py:233
  8.7 13.6 %constant_dynamic-slice_fusion.31 = (bf16[576,1,2304]{2,1,0:T(2,128)(2,1)}, bf16[576,1,2304]{2,1,0:T(2,128)(2,1)S(1)}) fusion(bf16[576,2,2304]{2,1,0:T(2,128)(2,1)} %reshape.404, s32[]{:T(128)S(6)} %select_n.328, s32[]{:T(128)S(6)} %select_n.329), kind=kLoop, calls=%fused_computation.296 | loop fusion | bytes 10616840 | tf_op jit(solution)/shard_map/jit(dynamic_index_in_dim)/dynamic_slice | solution.py:45
  24.7 2.6 collective-permute-start.14
  27.4 4.5 fusion.115
  41.6 2.7 collective-permute-start.17
  56.0 4.9 broadcast_select_fusion.1
  60.9 4.1 fusion.1
  65.3 2.7 attention_forward.1
  71.4 2.4 bitcast_select_fusion.1
  74.0 5.5 %multiply_convert_fusion = (bf16[512,2304]{1,0:T(8,128)(2,1)}, f32[512,2304]{1,0:T(8,128)S(1)}) fusion(f32[2304]{0:T(1024)S(1)} %copy-done.99, bf16[576,2304]{1,0:T(8,128)(2,1)S(1)} %get-tuple-element.99, bf16[576,2304]{1,0:T(8,128)(2,1)S(1)} %get-tuple-element.98, bf16[256,1152]{1,0:T(8,128)(2,1)S(1)} %collective-permute-done.4, ...), kind=kOutput, calls=%fused_computation.16 | convolution fusion | flops 2742681600 | bytes 13575168 | tf_op jit(solution)/shard_map/dot_general | solution.py:29
  79.5 6.1 %convert_reduce_fusion = (f32[2304]{0:T(1024)S(1)}, bf16[512,2304]{1,0:T(8,128)(2,1)S(1)}) fusion(f32[512,2304]{1,0:T(8,128)S(1)} %get-tuple-element.145, bf16[2304,1152]{1,0:T(8,128)(2,1)S(1)} %bitcast.410, bf16[256,1152]{1,0:T(8,128)(2,1)S(1)} %copy-done.66, bf16[256,1152]{1,0:T(8,128)(2,1)S(1)} %copy-done.46), kind=kOutput, calls=%fused_computation.15 | convolution fusion | flops 2746218240 | bytes 13575168 | tf_op jit(solution)/shard_map/dot_general | solution.py:37
  85.6 3.2 fusion.9
  88.9 3.0 fusion.53
  94.3 2.7 slice.174
  97.0 4.9 fusion.136
  110.9 2.9 fusion.32
  113.8 7.9 %collective-permute-done.63 = bf16[2,2,2,16,2304]{4,3,0,1,2:T(8,128)(2,1)} collective-permute-done((bf16[2,2,2,16,2304]{4,3,0,1,2:T(8,128)(2,1)}, bf16[2,2,2,16,2304]{4,3,0,1,2:T(8,128)(2,1)}, u32[]{:S(2)}, u32[]{:S(2)}) %collective-permute-start.63) | collective-permute-done | bytes 589856 | tf_op jit(solution)/shard_map/ppermute | solution.py:154
  124.1 7.9 %collective-permute-done.64 = bf16[2,2,16,2304]{3,2,0,1:T(8,128)(2,1)S(1)} collective-permute-done((bf16[2,2,16,2304]{3,2,0,1:T(8,128)(2,1)S(1)}, bf16[2,2,16,2304]{3,2,0,1:T(8,128)(2,1)S(1)}, u32[]{:S(2)}, u32[]{:S(2)}) %collective-permute-start.64) | collective-permute-done | bytes 294944 | tf_op jit(solution)/shard_map/ppermute | solution.py:154
  133.6 18.7 %collective-permute-done.59 = bf16[2,2,2,24,2304]{4,3,0,2,1:T(8,128)(2,1)S(1)} collective-permute-done((bf16[2,2,2,24,2304]{4,3,0,2,1:T(8,128)(2,1)S(1)}, bf16[2,2,2,24,2304]{4,3,0,2,1:T(8,128)(2,1)S(1)}, u32[]{:S(2)}, u32[]{:S(2)}) %collective-permute-start.59) | collective-permute-done | bytes 884768 | tf_op jit(solution)/shard_map/ppermute | solution.py:154
  154.0 3.4 collective-permute-done.65
  160.4 3.2 collective-permute-done.66
  164.9 2.5 multiply_reduce_fusion.1
  173.3 6.8 %attention_backward.1 = (bf16[256,1152]{1,0:T(8,128)(2,1)S(1)}, bf16[256,1152]{1,0:T(8,128)(2,1)S(1)}, bf16[256,1152]{1,0:T(8,128)(2,1)S(1)}) custom-call(bf16[256,1152]{1,0:T(8,128)(2,1)S(1)} %get-tuple-element.108.q_ref, bf16[256,1152]{1,0:T(8,128)(2,1)S(1)} %slice.219.k_ref, bf16[256,1152]{1,0:T(8,128)(2,1)S(1)} %get-tuple-element.107.v_ref, ...), custom_call_target="tpu_custom_call" | custom-call | flops 5368709120 | bytes 4128768 | tf_op jit(solution)/shard_map/attention_backward/pallas_call | solution.py:125
  186.0 2.7 copy.110
  188.7 6.5 %fusion.31 = (f32[256]{0:T(256)S(1)}, f32[256,1152]{1,0:T(8,128)S(1)}) fusion(f32[1152]{0:T(1024)S(1)} %get-tuple-element.86, f32[256]{0:T(256)S(1)} %broadcast_multiply_fusion.1, bf16[128,1152]{1,0:T(8,128)(2,1)S(1)} %copy-done.16, bf16[128,1152]{1,0:T(8,128)(2,1)S(1)} %copy-done.7, bf16[256,3456]{1,0:T(8,128)(2,1)} %constant_dynamic-update-slice_fusion, ...), kind=kOutput, calls=%fused_computation.69 | convolution fusion | flops 2056716032 | bytes 11508224 | tf_op jit(solution)/shard_map/dot_general | solution.py:37
  205.5 5.4 %fusion.137 = f32[2,576]{1,0:T(2,128)S(1)} fusion(bf16[2,6912]{1,0:T(2,128)(2,1)S(1)} %pad_maximum_fusion.25, bf16[576,6912]{1,0:T(8,128)(2,1)} %param.17), kind=kOutput, calls=%fused_computation.391 | convolution fusion | flops 15925248 | bytes 7994880 | tf_op jit(solution)/shard_map/dot_general | solution.py:37
  216.0 2.7 collective-permute-done.23
  222.7 3.4 collective-permute-done.24
  234.0 3.8 collective-permute-done.20
  247.3 5.4 %collective-permute-done.21 = bf16[16,3456]{1,0:T(8,128)(2,1)} collective-permute-done((bf16[16,3456]{1,0:T(8,128)(2,1)S(1)}, bf16[16,3456]{1,0:T(8,128)(2,1)}, u32[]{:S(2)}, u32[]{:S(2)}) %collective-permute-start.21) | collective-permute-done | bytes 110624 | tf_op jit(solution)/shard_map/ppermute | solution.py:199
  252.7 2.9 concatenate.184
  265.2 4.4 collective-permute-done.61
  269.7 5.7 %collective-permute-done.51 = bf16[2,2,2,16,576]{4,3,0,1,2:T(8,128)(2,1)S(1)} collective-permute-done((bf16[2,2,2,16,576]{4,3,0,1,2:T(8,128)(2,1)S(1)}, bf16[2,2,2,16,576]{4,3,0,1,2:T(8,128)(2,1)S(1)}, u32[]{:S(2)}, u32[]{:S(2)}) %collective-permute-start.51) | collective-permute-done | bytes 147488 | tf_op jit(solution)/shard_map/ppermute | solution.py:154
  276.6 5.7 %collective-permute-done.62 = bf16[24,2304]{1,0:T(8,128)(2,1)S(1)} collective-permute-done((bf16[24,2304]{1,0:T(8,128)(2,1)S(1)}, bf16[24,2304]{1,0:T(8,128)(2,1)S(1)}, u32[]{:S(2)}, u32[]{:S(2)}) %collective-permute-start.62) | collective-permute-done | bytes 110624 | tf_op jit(solution)/shard_map/ppermute | solution.py:154
  283.8 2.9 collective-permute-done.52
  288.3 5.1 %collective-permute-done.47 = bf16[2,2,2,24,576]{4,3,0,2,1:T(8,128)(2,1)S(1)} collective-permute-done((bf16[2,2,2,24,576]{4,3,0,2,1:T(8,128)(2,1)S(1)}, bf16[2,2,2,24,576]{4,3,0,2,1:T(8,128)(2,1)S(1)}, u32[]{:S(2)}, u32[]{:S(2)}) %collective-permute-start.47) | collective-permute-done | bytes 221216 | tf_op jit(solution)/shard_map/ppermute | solution.py:154
  295.0 2.5 collective-permute-done.53
  297.6 4.6 collective-permute-done.54
  305.4 7.0 %collective-permute-done.56 = bf16[2,2,32,2304]{3,2,1,0:T(8,128)(2,1)S(1)} collective-permute-done((bf16[2,2,32,2304]{3,2,1,0:T(8,128)(2,1)S(1)}, bf16[2,2,32,2304]{3,2,1,0:T(8,128)(2,1)S(1)}, u32[]{:S(2)}, u32[]{:S(2)}) %collective-permute-start.56) | collective-permute-done | bytes 589856 | tf_op jit(solution)/shard_map/ppermute | solution.py:154
  318.9 2.7 collective-permute-done.49
  323.1 3.8 collective-permute-done.44
  327.4 4.1 collective-permute-done.45
  332.5 3.9 collective-permute-done.50
  337.3 4.3 collective-permute-done.46
  342.2 3.8 fusion.15
  357.2 3.7 collective-permute-done.58
  361.8 3.3 convolution_convert_fusion
  365.2 3.2 broadcast_select_fusion.3
  368.4 2.8 pad_maximum_fusion.2
  371.2 8.4 %copy.127 = bf16[4608,576]{1,0:T(8,128)(2,1)} copy(bf16[4608,576]{0,1:T(8,128)(2,1)} %pad_maximum_fusion.2) | data formatting | bytes 10616832 | tf_op jit(solution)/shard_map/concatenate | solution.py:51
  381.0 3.0 slice.178
  394.2 2.4 copy.150
  396.6 2.6 copy.128
  399.1 2.6 dynamic-slice_bitcast_fusion
  404.7 7.9 %collective-permute-done.39 = bf16[2,16,1728]{2,1,0:T(8,128)(2,1)S(1)} collective-permute-done((bf16[2,16,1728]{2,1,0:T(8,128)(2,1)S(1)}, bf16[2,16,1728]{2,1,0:T(8,128)(2,1)S(1)}, u32[]{:S(2)}, u32[]{:S(2)}) %collective-permute-start.39) | collective-permute-done | bytes 110624 | tf_op jit(solution)/shard_map/ppermute | solution.py:154
  412.7 3.7 collective-permute-start.40
  430.5 3.0 collective-permute-done.35
  435.1 3.4 collective-permute-start.36
  447.2 2.4 collective-permute-done.78
  453.0 5.2 %collective-permute-done.79 = bf16[64,576]{0,1:T(8,128)(2,1)S(1)} collective-permute-done((bf16[64,576]{0,1:T(8,128)(2,1)S(1)}, bf16[64,576]{0,1:T(8,128)(2,1)S(1)}, u32[]{:S(2)}, u32[]{:S(2)}) %collective-permute-start.79) | collective-permute-done | bytes 73760 | tf_op jit(solution)/shard_map/ppermute | solution.py:154
  460.7 3.7 collective-permute-done.31
  467.0 6.4 %collective-permute-done.32 = bf16[32,1728]{1,0:T(8,128)(2,1)} collective-permute-done((bf16[32,1728]{1,0:T(8,128)(2,1)}, bf16[32,1728]{1,0:T(8,128)(2,1)}, u32[]{:S(2)}, u32[]{:S(2)}) %collective-permute-start.32) | collective-permute-done | bytes 110624 | tf_op jit(solution)/shard_map/ppermute | solution.py:154
  478.7 6.2 %collective-permute-done.70 = bf16[2,128,576]{1,2,0:T(8,128)(2,1)S(1)} collective-permute-done((bf16[2,128,576]{1,2,0:T(8,128)(2,1)S(1)}, bf16[2,128,576]{1,2,0:T(8,128)(2,1)S(1)}, u32[]{:S(2)}, u32[]{:S(2)}) %collective-permute-start.70) | collective-permute-done | bytes 294944 | tf_op jit(solution)/shard_map/ppermute | solution.py:154
  485.1 6.6 %collective-permute-done.71 = bf16[128,576]{0,1:T(8,128)(2,1)S(1)} collective-permute-done((bf16[128,576]{0,1:T(8,128)(2,1)S(1)}, bf16[128,576]{0,1:T(8,128)(2,1)S(1)}, u32[]{:S(2)}, u32[]{:S(2)}) %collective-permute-start.71) | collective-permute-done | bytes 147488 | tf_op jit(solution)/shard_map/ppermute | solution.py:154
  (590 shorter events, 192.3 us)
Async XLA Ops:
  24.2 47.1 %collective-permute-start.5 = (bf16[576,2304]{1,0:T(8,128)(2,1)}, bf16[576,2304]{1,0:T(8,128)(2,1)}, u32[]{:S(2)}, u32[]{:S(2)}) collective-permute-start(bf16[576,2304]{1,0:T(8,128)(2,1)} %bitcast.363), channel_id=1, source_target_pairs={{0,1},{1,0},{2,3},{3,2},{4,5},{5,4},{6,7},{7,6},{8,9},{9,8},{10,11... | collective-permute-start | bytes 7962632 | tf_op jit(solution)/shard_map/ppermute | solution.py:41
  24.7 8.9 %collective-permute-start.14 = (bf16[2,1152]{1,0:T(2,128)(2,1)S(1)}, bf16[2,1152]{1,0:T(2,128)(2,1)S(1)}, u32[]{:S(2)}, u32[]{:S(2)}) collective-permute-start(bf16[2,1152]{1,0:T(2,128)(2,1)S(1)} %fusion.105), channel_id=1, source_target_pairs={{0,2},{2,0},{4,6},{6,4},{8,10},{10,8},{12,14},{14,12},{16,18},{18,... | collective-permute-start | bytes 13832 | tf_op jit(solution)/shard_map/ppermute | solution.py:199
  31.9 9.8 %collective-permute-start.1 = (f32[2,6912]{1,0:T(2,128)S(1)}, f32[2,6912]{1,0:T(2,128)S(1)}, u32[]{:S(2)}, u32[]{:S(2)}) collective-permute-start(f32[2,6912]{1,0:T(2,128)S(1)} %fusion.115), channel_id=1, source_target_pairs={{0,1},{1,0},{2,3},{3,2},{4,5},{5,4},{6,7},{7,6},{8,9},{9,8},{10,11... | collective-permute-start | bytes 165896 | tf_op jit(solution)/shard_map/ppermute | solution.py:41
  32.2 16.0 %collective-permute-start = (bf16[128,1152]{1,0:T(8,128)(2,1)S(1)}, bf16[128,1152]{1,0:T(8,128)(2,1)S(1)}, u32[]{:S(2)}, u32[]{:S(2)}) collective-permute-start(bf16[128,1152]{1,0:T(8,128)(2,1)S(1)} %get-tuple-element.130), channel_id=1, source_target_pairs={{0,1},{1,0},{2,3},{3,2},{4,5},{5,4},{6,7},{7,6},{8,9},{9,8},{10,11... | collective-permute-start | bytes 884744 | tf_op jit(solution)/shard_map/ppermute | solution.py:41
  32.6 23.4 %collective-permute-start.2 = (bf16[576,3456]{1,0:T(8,128)(2,1)}, bf16[576,3456]{1,0:T(8,128)(2,1)}, u32[]{:S(2)}, u32[]{:S(2)}) collective-permute-start(bf16[576,3456]{1,0:T(8,128)(2,1)} %param.19), channel_id=1, source_target_pairs={{0,1},{1,0},{2,3},{3,2},{4,5},{5,4},{6,7},{7,6},{8,9},{9,8},{10,11... | collective-permute-start | bytes 11943944 | tf_op jit(solution)/shard_map/ppermute | solution.py:41
  41.6 6.8 %collective-permute-start.8 = (bf16[128,1152]{1,0:T(8,128)(2,1)S(1)}, bf16[128,1152]{1,0:T(8,128)(2,1)S(1)}, u32[]{:S(2)}, u32[]{:S(2)}) collective-permute-start(bf16[128,1152]{1,0:T(8,128)(2,1)S(1)} %get-tuple-element.128), channel_id=1, source_target_pairs={{0,1},{1,0},{2,3},{3,2},{4,5},{5,4},{6,7},{7,6},{8,9},{9,8},{10,11... | collective-permute-start | bytes 884744 | tf_op jit(solution)/shard_map/ppermute | solution.py:41
  41.6 5.7 %collective-permute-start.17 = (bf16[16,1152]{1,0:T(8,128)(2,1)S(1)}, bf16[16,1152]{1,0:T(8,128)(2,1)S(1)}, u32[]{:S(2)}, u32[]{:S(2)}) collective-permute-start(bf16[16,1152]{1,0:T(8,128)(2,1)S(1)} %pad_maximum_fusion.24), channel_id=1, source_target_pairs={{0,16},{2,18},{4,20},{6,22},{8,24},{10,26},{12,28},{14,30},{16,0},... | collective-permute-start | bytes 110600 | tf_op jit(solution)/shard_map/ppermute | solution.py:199
  47.4 6.6 %collective-permute-start.3 = (bf16[576,1152]{1,0:T(8,128)(2,1)}, bf16[576,1152]{1,0:T(8,128)(2,1)}, u32[]{:S(2)}, u32[]{:S(2)}) collective-permute-start(bf16[576,1152]{1,0:T(8,128)(2,1)} %param.21), channel_id=1, source_target_pairs={{0,1},{1,0},{2,3},{3,2},{4,5},{5,4},{6,7},{7,6},{8,9},{9,8},{10,11... | collective-permute-start | bytes 3981320 | tf_op jit(solution)/shard_map/ppermute | solution.py:41
  51.5 290.7 %collective-permute-start.27 = (bf16[256,1152]{1,0:T(8,128)(2,1)}, bf16[256,1152]{1,0:T(8,128)(2,1)}, u32[]{:S(2)}, u32[]{:S(2)}) collective-permute-start(bf16[256,1152]{1,0:T(8,128)(2,1)} %fusion.28), channel_id=1, source_target_pairs={{0,1},{1,0},{2,3},{3,2},{4,5},{5,4},{6,7},{7,6},{8,9},{9,8},{10,11... | collective-permute-start | bytes 1769480 | tf_op jit(solution)/shard_map/ppermute | solution.py:41
  73.8 184.0 %collective-permute-start.41 = (bf16[256,1152]{1,0:T(8,128)(2,1)S(1)}, bf16[256,1152]{1,0:T(8,128)(2,1)}, u32[]{:S(2)}, u32[]{:S(2)}) collective-permute-start(bf16[256,1152]{1,0:T(8,128)(2,1)S(1)} %get-tuple-element.18), channel_id=1, source_target_pairs={{0,1},{1,0},{2,3},{3,2},{4,5},{5,4},{6,7},{7,6},{8,9},{9,8},{10,11... | collective-permute-start | bytes 1769480 | tf_op jit(solution)/shard_map/ppermute | solution.py:41
  101.9 259.9 %collective-permute-start.67 = (bf16[512,2304]{1,0:T(8,128)(2,1)}, bf16[512,2304]{1,0:T(8,128)(2,1)}, u32[]{:S(2)}, u32[]{:S(2)}) collective-permute-start(bf16[512,2304]{1,0:T(8,128)(2,1)} %get-tuple-element.144), channel_id=1, source_target_pairs={{0,1},{1,0},{2,3},{3,2},{4,5},{5,4},{6,7},{7,6},{8,9},{9,8},{10,11... | collective-permute-start | bytes 7077896 | tf_op jit(solution)/shard_map/ppermute | solution.py:41
  104.8 59.5 %collective-permute-start.10 = (f32[256,1152]{1,0:T(8,128)}, f32[256,1152]{1,0:T(8,128)}, u32[]{:S(2)}, u32[]{:S(2)}) collective-permute-start(f32[256,1152]{1,0:T(8,128)} %slice.165), channel_id=1, source_target_pairs={{0,1},{1,0},{2,3},{3,2},{4,5},{5,4},{6,7},{7,6},{8,9},{9,8},{10,11... | collective-permute-start | bytes 3538952 | tf_op jit(solution)/shard_map/ppermute | solution.py:41
  105.8 16.0 %collective-permute-start.63 = (bf16[2,2,2,16,2304]{4,3,0,1,2:T(8,128)(2,1)}, bf16[2,2,2,16,2304]{4,3,0,1,2:T(8,128)(2,1)}, u32[]{:S(2)}, u32[]{:S(2)}) collective-permute-start(bf16[2,2,2,16,2304]{4,3,0,1,2:T(8,128)(2,1)} %fusion.57), channel_id=1, source_target_pairs={{0,8},{2,10},{4,12},{6,14},{8,0},{10,2},{12,4},{14,6},{16,24},{18,... | collective-permute-start | bytes 1769480 | tf_op jit(solution)/shard_map/ppermute | solution.py:154
  123.4 8.6 %collective-permute-start.64 = (bf16[2,2,16,2304]{3,2,0,1:T(8,128)(2,1)S(1)}, bf16[2,2,16,2304]{3,2,0,1:T(8,128)(2,1)S(1)}, u32[]{:S(2)}, u32[]{:S(2)}) collective-permute-start(bf16[2,2,16,2304]{3,2,0,1:T(8,128)(2,1)S(1)} %dynamic-slice_bitcast_fusion.15), channel_id=1, source_target_pairs={{0,2},{2,0},{4,6},{6,4},{8,10},{10,8},{12,14},{14,12},{16,18},{18,... | collective-permute-start | bytes 884744 | tf_op jit(solution)/shard_map/ppermute | solution.py:154
  132.0 20.3 %collective-permute-start.59 = (bf16[2,2,2,24,2304]{4,3,0,2,1:T(8,128)(2,1)S(1)}, bf16[2,2,2,24,2304]{4,3,0,2,1:T(8,128)(2,1)S(1)}, u32[]{:S(2)}, u32[]{:S(2)}) collective-permute-start(bf16[2,2,2,24,2304]{4,3,0,2,1:T(8,128)(2,1)S(1)} %fusion.51), channel_id=1, source_target_pairs={{0,4},{2,6},{4,0},{6,2},{8,12},{10,14},{12,8},{14,10},{16,20},{18,... | collective-permute-start | bytes 2654216 | tf_op jit(solution)/shard_map/ppermute | solution.py:154
  152.3 5.1 %collective-permute-start.65 = (bf16[2,16,2304]{2,1,0:T(8,128)(2,1)S(1)}, bf16[2,16,2304]{2,1,0:T(8,128)(2,1)S(1)}, u32[]{:S(2)}, u32[]{:S(2)}) collective-permute-start(bf16[2,16,2304]{2,1,0:T(8,128)(2,1)S(1)} %dynamic-slice_bitcast_fusion.31), channel_id=1, source_target_pairs={{0,4},{2,6},{4,0},{6,2},{8,12},{10,14},{12,8},{14,10},{16,20},{18,... | collective-permute-start | bytes 442376 | tf_op jit(solution)/shard_map/ppermute | solution.py:154
  157.5 6.1 %collective-permute-start.66 = (bf16[16,2304]{1,0:T(8,128)(2,1)S(1)}, bf16[16,2304]{1,0:T(8,128)(2,1)S(1)}, u32[]{:S(2)}, u32[]{:S(2)}) collective-permute-start(bf16[16,2304]{1,0:T(8,128)(2,1)S(1)} %dynamic-slice_bitcast_fusion.40), channel_id=1, source_target_pairs={{0,16},{2,18},{4,20},{6,22},{8,24},{10,26},{12,28},{14,30},{16,0},... | collective-permute-start | bytes 221192 | tf_op jit(solution)/shard_map/ppermute | solution.py:154
  164.3 37.3 %collective-permute-start.55 = (bf16[2,2,2,32,2304]{4,3,2,1,0:T(8,128)(2,1)}, bf16[2,2,2,32,2304]{4,3,2,1,0:T(8,128)(2,1)}, u32[]{:S(2)}, u32[]{:S(2)}) collective-permute-start(bf16[2,2,2,32,2304]{4,3,2,1,0:T(8,128)(2,1)} %fusion.32), channel_id=1, source_target_pairs={{0,2},{2,0},{4,6},{6,4},{8,10},{10,8},{12,14},{14,12},{16,18},{18,... | collective-permute-start | bytes 3538952 | tf_op jit(solution)/shard_map/ppermute | solution.py:154
  167.9 76.0 %collective-permute-start.60 = (bf16[2,2,24,2304]{3,2,0,1:T(8,128)(2,1)}, bf16[2,2,24,2304]{3,2,0,1:T(8,128)(2,1)}, u32[]{:S(2)}, u32[]{:S(2)}) collective-permute-start(bf16[2,2,24,2304]{3,2,0,1:T(8,128)(2,1)} %dynamic-slice_bitcast_fusion.8), channel_id=1, source_target_pairs={{0,8},{2,10},{4,12},{6,14},{8,0},{10,2},{12,4},{14,6},{16,24},{18,... | collective-permute-start | bytes 1327112 | tf_op jit(solution)/shard_map/ppermute | solution.py:154
  213.4 5.3 %collective-permute-start.23 = (f32[2,2,2,1008]{3,2,1,0:T(2,128)S(1)}, f32[2,2,2,1008]{3,2,1,0:T(2,128)S(1)}, u32[]{:S(2)}, u32[]{:S(2)}) collective-permute-start(f32[2,2,2,1008]{3,2,1,0:T(2,128)S(1)} %dynamic-slice_bitcast_fusion.45), channel_id=1, source_target_pairs={{0,16},{2,18},{4,20},{6,22},{8,24},{10,26},{12,28},{14,30},{16,0},... | collective-permute-start | bytes 96776 | tf_op jit(solution)/shard_map/ppermute | solution.py:190
  241.4 16.9 %collective-permute-start.42 = (bf16[256,576]{0,1:T(8,128)(2,1)}, bf16[256,576]{0,1:T(8,128)(2,1)}, u32[]{:S(2)}, u32[]{:S(2)}) collective-permute-start(bf16[256,576]{0,1:T(8,128)(2,1)} %get-tuple-element.126), channel_id=1, source_target_pairs={{0,1},{1,0},{2,3},{3,2},{4,5},{5,4},{6,7},{7,6},{8,9},{9,8},{10,11... | collective-permute-start | bytes 884744 | tf_op jit(solution)/shard_map/ppermute | solution.py:41
  243.9 8.8 %collective-permute-start.21 = (bf16[16,3456]{1,0:T(8,128)(2,1)S(1)}, bf16[16,3456]{1,0:T(8,128)(2,1)}, u32[]{:S(2)}, u32[]{:S(2)}) collective-permute-start(bf16[16,3456]{1,0:T(8,128)(2,1)S(1)} %pad_maximum_fusion.22), channel_id=1, source_target_pairs={{0,16},{2,18},{4,20},{6,22},{8,24},{10,26},{12,28},{14,30},{16,0},... | collective-permute-start | bytes 331784 | tf_op jit(solution)/shard_map/ppermute | solution.py:199
  252.7 8.4 %collective-permute-start.7 = (bf16[1,128,1152]{2,1,0:T(8,128)(2,1)}, bf16[1,128,1152]{2,1,0:T(8,128)(2,1)}, u32[]{:S(2)}, u32[]{:S(2)}) collective-permute-start(bf16[1,128,1152]{2,1,0:T(8,128)(2,1)} %slice_bitcast_fusion.2), channel_id=1, source_target_pairs={{0,1},{1,0},{2,3},{3,2},{4,5},{5,4},{6,7},{7,6},{8,9},{9,8},{10,11... | collective-permute-start | bytes 884744 | tf_op jit(solution)/shard_map/ppermute | solution.py:41
  257.8 45.9 %collective-permute-start.11 = (f32[1,128,1152]{2,1,0:T(8,128)}, f32[1,128,1152]{2,1,0:T(8,128)S(1)}, u32[]{:S(2)}, u32[]{:S(2)}) collective-permute-start(f32[1,128,1152]{2,1,0:T(8,128)} %slice_bitcast_fusion), channel_id=1, source_target_pairs={{0,1},{1,0},{2,3},{3,2},{4,5},{5,4},{6,7},{7,6},{8,9},{9,8},{10,11... | collective-permute-start | bytes 1769480 | tf_op jit(solution)/shard_map/ppermute | solution.py:41
  258.3 83.9 %collective-permute-start.28 = (bf16[256,1728]{0,1:T(8,128)(2,1)}, bf16[256,1728]{0,1:T(8,128)(2,1)S(1)}, u32[]{:S(2)}, u32[]{:S(2)}) collective-permute-start(bf16[256,1728]{0,1:T(8,128)(2,1)} %get-tuple-element.116), channel_id=1, source_target_pairs={{0,1},{1,0},{2,3},{3,2},{4,5},{5,4},{6,7},{7,6},{8,9},{9,8},{10,11... | collective-permute-start | bytes 2654216 | tf_op jit(solution)/shard_map/ppermute | solution.py:41
  261.8 7.8 %collective-permute-start.61 = (bf16[2,24,2304]{2,1,0:T(8,128)(2,1)S(1)}, bf16[2,24,2304]{2,1,0:T(8,128)(2,1)S(1)}, u32[]{:S(2)}, u32[]{:S(2)}) collective-permute-start(bf16[2,24,2304]{2,1,0:T(8,128)(2,1)S(1)} %copy-done.70), channel_id=1, source_target_pairs={{0,2},{2,0},{4,6},{6,4},{8,10},{10,8},{12,14},{14,12},{16,18},{18,... | collective-permute-start | bytes 663560 | tf_op jit(solution)/shard_map/ppermute | solution.py:154
  269.6 5.8 %collective-permute-start.51 = (bf16[2,2,2,16,576]{4,3,0,1,2:T(8,128)(2,1)S(1)}, bf16[2,2,2,16,576]{4,3,0,1,2:T(8,128)(2,1)S(1)}, u32[]{:S(2)}, u32[]{:S(2)}) collective-permute-start(bf16[2,2,2,16,576]{4,3,0,1,2:T(8,128)(2,1)S(1)} %fusion.86), channel_id=1, source_target_pairs={{0,8},{2,10},{4,12},{6,14},{8,0},{10,2},{12,4},{14,6},{16,24},{18,... | collective-permute-start | bytes 442376 | tf_op jit(solution)/shard_map/ppermute | solution.py:154
  275.3 7.0 %collective-permute-start.62 = (bf16[24,2304]{1,0:T(8,128)(2,1)S(1)}, bf16[24,2304]{1,0:T(8,128)(2,1)S(1)}, u32[]{:S(2)}, u32[]{:S(2)}) collective-permute-start(bf16[24,2304]{1,0:T(8,128)(2,1)S(1)} %dynamic-slice_bitcast_fusion.36), channel_id=1, source_target_pairs={{0,16},{2,18},{4,20},{6,22},{8,24},{10,26},{12,28},{14,30},{16,0},... | collective-permute-start | bytes 331784 | tf_op jit(solution)/shard_map/ppermute | solution.py:154
  282.3 4.4 collective-permute-start.52
  286.8 6.6 %collective-permute-start.47 = (bf16[2,2,2,24,576]{4,3,0,2,1:T(8,128)(2,1)S(1)}, bf16[2,2,2,24,576]{4,3,0,2,1:T(8,128)(2,1)S(1)}, u32[]{:S(2)}, u32[]{:S(2)}) collective-permute-start(bf16[2,2,2,24,576]{4,3,0,2,1:T(8,128)(2,1)S(1)} %fusion.83), channel_id=1, source_target_pairs={{0,4},{2,6},{4,0},{6,2},{8,12},{10,14},{12,8},{14,10},{16,20},{18,... | collective-permute-start | bytes 663560 | tf_op jit(solution)/shard_map/ppermute | solution.py:154
  297.4 4.7 collective-permute-start.54
  302.2 10.2 %collective-permute-start.56 = (bf16[2,2,32,2304]{3,2,1,0:T(8,128)(2,1)S(1)}, bf16[2,2,32,2304]{3,2,1,0:T(8,128)(2,1)S(1)}, u32[]{:S(2)}, u32[]{:S(2)}) collective-permute-start(bf16[2,2,32,2304]{3,2,1,0:T(8,128)(2,1)S(1)} %copy-done.61), channel_id=1, source_target_pairs={{0,4},{2,6},{4,0},{6,2},{8,12},{10,14},{12,8},{14,10},{16,20},{18,... | collective-permute-start | bytes 1769480 | tf_op jit(solution)/shard_map/ppermute | solution.py:154
  303.7 10.3 %collective-permute-start.43 = (bf16[2,2,2,32,576]{4,3,2,1,0:T(8,128)(2,1)S(1)}, bf16[2,2,2,32,576]{4,3,2,1,0:T(8,128)(2,1)S(1)}, u32[]{:S(2)}, u32[]{:S(2)}) collective-permute-start(bf16[2,2,2,32,576]{4,3,2,1,0:T(8,128)(2,1)S(1)} %fusion.79), channel_id=1, source_target_pairs={{0,2},{2,0},{4,6},{6,4},{8,10},{10,8},{12,14},{14,12},{16,18},{18,... | collective-permute-start | bytes 884744 | tf_op jit(solution)/shard_map/ppermute | solution.py:154
  312.4 4.9 collective-permute-start.48
  314.0 39.1 %collective-permute-start.57 = (bf16[2,32,2304]{2,1,0:T(8,128)(2,1)S(1)}, bf16[2,32,2304]{2,1,0:T(8,128)(2,1)S(1)}, u32[]{:S(2)}, u32[]{:S(2)}) collective-permute-start(bf16[2,32,2304]{2,1,0:T(8,128)(2,1)S(1)} %dynamic-slice_bitcast_fusion.16), channel_id=1, source_target_pairs={{0,8},{2,10},{4,12},{6,14},{8,0},{10,2},{12,4},{14,6},{16,24},{18,... | collective-permute-start | bytes 884744 | tf_op jit(solution)/shard_map/ppermute | solution.py:154
  321.6 5.3 %collective-permute-start.44 = (bf16[2,2,32,576]{3,2,1,0:T(8,128)(2,1)S(1)}, bf16[2,2,32,576]{3,2,1,0:T(8,128)(2,1)S(1)}, u32[]{:S(2)}, u32[]{:S(2)}) collective-permute-start(bf16[2,2,32,576]{3,2,1,0:T(8,128)(2,1)S(1)} %dynamic-slice_bitcast_fusion.27), channel_id=1, source_target_pairs={{0,4},{2,6},{4,0},{6,2},{8,12},{10,14},{12,8},{14,10},{16,20},{18,... | collective-permute-start | bytes 442376 | tf_op jit(solution)/shard_map/ppermute | solution.py:154
  327.0 4.5 collective-permute-start.45
  331.5 4.9 collective-permute-start.50
  336.4 5.1 %collective-permute-start.46 = (bf16[32,576]{1,0:T(8,128)(2,1)S(1)}, bf16[32,576]{1,0:T(8,128)(2,1)S(1)}, u32[]{:S(2)}, u32[]{:S(2)}) collective-permute-start(bf16[32,576]{1,0:T(8,128)(2,1)S(1)} %dynamic-slice_bitcast_fusion.44), channel_id=1, source_target_pairs={{0,16},{2,18},{4,20},{6,22},{8,24},{10,26},{12,28},{14,30},{16,0},... | collective-permute-start | bytes 110600 | tf_op jit(solution)/shard_map/ppermute | solution.py:154
  349.0 39.4 %collective-permute-start.37 = (bf16[2,2,2,16,1728]{4,3,0,1,2:T(8,128)(2,1)}, bf16[2,2,2,16,1728]{4,3,0,1,2:T(8,128)(2,1)}, u32[]{:S(2)}, u32[]{:S(2)}) collective-permute-start(bf16[2,2,2,16,1728]{4,3,0,1,2:T(8,128)(2,1)} %fusion.74), channel_id=1, source_target_pairs={{0,8},{2,10},{4,12},{6,14},{8,0},{10,2},{12,4},{14,6},{16,24},{18,... | collective-permute-start | bytes 1327112 | tf_op jit(solution)/shard_map/ppermute | solution.py:154
  351.5 50.8 %collective-permute-start.33 = (bf16[2,2,2,24,1728]{4,3,0,2,1:T(8,128)(2,1)}, bf16[2,2,2,24,1728]{4,3,0,2,1:T(8,128)(2,1)}, u32[]{:S(2)}, u32[]{:S(2)}) collective-permute-start(bf16[2,2,2,24,1728]{4,3,0,2,1:T(8,128)(2,1)} %fusion.54), channel_id=1, source_target_pairs={{0,4},{2,6},{4,0},{6,2},{8,12},{10,14},{12,8},{14,10},{16,20},{18,... | collective-permute-start | bytes 1990664 | tf_op jit(solution)/shard_map/ppermute | solution.py:154
  353.2 7.7 %collective-permute-start.58 = (bf16[32,2304]{1,0:T(8,128)(2,1)S(1)}, bf16[32,2304]{1,0:T(8,128)(2,1)S(1)}, u32[]{:S(2)}, u32[]{:S(2)}) collective-permute-start(bf16[32,2304]{1,0:T(8,128)(2,1)S(1)} %dynamic-slice_bitcast_fusion.32), channel_id=1, source_target_pairs={{0,16},{2,18},{4,20},{6,22},{8,24},{10,26},{12,28},{14,30},{16,0},... | collective-permute-start | bytes 442376 | tf_op jit(solution)/shard_map/ppermute | solution.py:154
  355.6 65.1 %collective-permute-start.29 = (bf16[2,2,2,32,1728]{4,3,2,1,0:T(8,128)(2,1)}, bf16[2,2,2,32,1728]{4,3,2,1,0:T(8,128)(2,1)}, u32[]{:S(2)}, u32[]{:S(2)}) collective-permute-start(bf16[2,2,2,32,1728]{4,3,2,1,0:T(8,128)(2,1)} %fusion.48), channel_id=1, source_target_pairs={{0,2},{2,0},{4,6},{6,4},{8,10},{10,8},{12,14},{14,12},{16,18},{18,... | collective-permute-start | bytes 2654216 | tf_op jit(solution)/shard_map/ppermute | solution.py:154
  387.1 36.2 %collective-permute-start.76 = (bf16[2,2,2,64,576]{4,3,2,1,0:T(8,128)(2,1)}, bf16[2,2,2,64,576]{4,3,2,1,0:T(8,128)(2,1)}, u32[]{:S(2)}, u32[]{:S(2)}) collective-permute-start(bf16[2,2,2,64,576]{4,3,2,1,0:T(8,128)(2,1)} %get-tuple-element.120), channel_id=1, source_target_pairs={{0,8},{2,10},{4,12},{6,14},{8,0},{10,2},{12,4},{14,6},{16,24},{18,... | collective-permute-start | bytes 1769480 | tf_op jit(solution)/shard_map/ppermute | solution.py:154
  390.0 11.7 %collective-permute-start.38 = (bf16[2,2,16,1728]{3,2,0,1:T(8,128)(2,1)S(1)}, bf16[2,2,16,1728]{3,2,0,1:T(8,128)(2,1)S(1)}, u32[]{:S(2)}, u32[]{:S(2)}) collective-permute-start(bf16[2,2,16,1728]{3,2,0,1:T(8,128)(2,1)S(1)} %dynamic-slice_bitcast_fusion.23), channel_id=1, source_target_pairs={{0,2},{2,0},{4,6},{6,4},{8,10},{10,8},{12,14},{14,12},{16,18},{18,... | collective-permute-start | bytes 663560 | tf_op jit(solution)/shard_map/ppermute | solution.py:154
  393.2 46.7 %collective-permute-start.72 = (bf16[2,2,2,96,576]{4,3,2,1,0:T(8,128)(2,1)}, bf16[2,2,2,96,576]{4,3,2,1,0:T(8,128)(2,1)}, u32[]{:S(2)}, u32[]{:S(2)}) collective-permute-start(bf16[2,2,2,96,576]{4,3,2,1,0:T(8,128)(2,1)} %get-tuple-element.112), channel_id=1, source_target_pairs={{0,4},{2,6},{4,0},{6,2},{8,12},{10,14},{12,8},{14,10},{16,20},{18,... | collective-permute-start | bytes 2654216 | tf_op jit(solution)/shard_map/ppermute | solution.py:154
  401.7 56.5 %collective-permute-start.68 = (bf16[2,2,2,128,576]{3,4,2,1,0:T(8,128)(2,1)}, bf16[2,2,2,128,576]{3,4,2,1,0:T(8,128)(2,1)}, u32[]{:S(2)}, u32[]{:S(2)}) collective-permute-start(bf16[2,2,2,128,576]{3,4,2,1,0:T(8,128)(2,1)} %dynamic-slice_bitcast_fusion), channel_id=1, source_target_pairs={{0,2},{2,0},{4,6},{6,4},{8,10},{10,8},{12,14},{14,12},{16,18},{18,... | collective-permute-start | bytes 3538952 | tf_op jit(solution)/shard_map/ppermute | solution.py:154
  402.4 10.2 %collective-permute-start.39 = (bf16[2,16,1728]{2,1,0:T(8,128)(2,1)S(1)}, bf16[2,16,1728]{2,1,0:T(8,128)(2,1)S(1)}, u32[]{:S(2)}, u32[]{:S(2)}) collective-permute-start(bf16[2,16,1728]{2,1,0:T(8,128)(2,1)S(1)} %dynamic-slice_bitcast_fusion.34), channel_id=1, source_target_pairs={{0,4},{2,6},{4,0},{6,2},{8,12},{10,14},{12,8},{14,10},{16,20},{18,... | collective-permute-start | bytes 331784 | tf_op jit(solution)/shard_map/ppermute | solution.py:154
  412.7 5.9 %collective-permute-start.40 = (bf16[16,1728]{1,0:T(8,128)(2,1)S(1)}, bf16[16,1728]{1,0:T(8,128)(2,1)S(1)}, u32[]{:S(2)}, u32[]{:S(2)}) collective-permute-start(bf16[16,1728]{1,0:T(8,128)(2,1)S(1)} %dynamic-slice_bitcast_fusion.42), channel_id=1, source_target_pairs={{0,16},{2,18},{4,20},{6,22},{8,24},{10,26},{12,28},{14,30},{16,0},... | collective-permute-start | bytes 165896 | tf_op jit(solution)/shard_map/ppermute | solution.py:154
  418.5 7.4 %collective-permute-start.34 = (bf16[2,2,24,1728]{3,2,0,1:T(8,128)(2,1)S(1)}, bf16[2,2,24,1728]{3,2,0,1:T(8,128)(2,1)}, u32[]{:S(2)}, u32[]{:S(2)}) collective-permute-start(bf16[2,2,24,1728]{3,2,0,1:T(8,128)(2,1)S(1)} %dynamic-slice_bitcast_fusion.9), channel_id=1, source_target_pairs={{0,8},{2,10},{4,12},{6,14},{8,0},{10,2},{12,4},{14,6},{16,24},{18,... | collective-permute-start | bytes 995336 | tf_op jit(solution)/shard_map/ppermute | solution.py:154
  423.0 22.9 %collective-permute-start.30 = (bf16[2,2,32,1728]{3,2,1,0:T(8,128)(2,1)}, bf16[2,2,32,1728]{3,2,1,0:T(8,128)(2,1)}, u32[]{:S(2)}, u32[]{:S(2)}) collective-permute-start(bf16[2,2,32,1728]{3,2,1,0:T(8,128)(2,1)} %dynamic-slice_bitcast_fusion.7), channel_id=1, source_target_pairs={{0,4},{2,6},{4,0},{6,2},{8,12},{10,14},{12,8},{14,10},{16,20},{18,... | collective-permute-start | bytes 1327112 | tf_op jit(solution)/shard_map/ppermute | solution.py:154
  427.7 5.7 %collective-permute-start.35 = (bf16[2,24,1728]{2,1,0:T(8,128)(2,1)}, bf16[2,24,1728]{2,1,0:T(8,128)(2,1)}, u32[]{:S(2)}, u32[]{:S(2)}) collective-permute-start(bf16[2,24,1728]{2,1,0:T(8,128)(2,1)} %dynamic-slice_bitcast_fusion.26), channel_id=1, source_target_pairs={{0,2},{2,0},{4,6},{6,4},{8,10},{10,8},{12,14},{14,12},{16,18},{18,... | collective-permute-start | bytes 497672 | tf_op jit(solution)/shard_map/ppermute | solution.py:154
  428.6 9.9 %collective-permute-start.77 = (bf16[2,2,64,576]{3,2,1,0:T(8,128)(2,1)S(1)}, bf16[2,2,64,576]{3,2,1,0:T(8,128)(2,1)S(1)}, u32[]{:S(2)}, u32[]{:S(2)}) collective-permute-start(bf16[2,2,64,576]{3,2,1,0:T(8,128)(2,1)S(1)} %bitcast.405), channel_id=1, source_target_pairs={{0,2},{2,0},{4,6},{6,4},{8,10},{10,8},{12,14},{14,12},{16,18},{18,... | collective-permute-start | bytes 884744 | tf_op jit(solution)/shard_map/ppermute | solution.py:154
  435.1 9.2 %collective-permute-start.36 = (bf16[24,1728]{1,0:T(8,128)(2,1)}, bf16[24,1728]{1,0:T(8,128)(2,1)}, u32[]{:S(2)}, u32[]{:S(2)}) collective-permute-start(bf16[24,1728]{1,0:T(8,128)(2,1)} %dynamic-slice_bitcast_fusion.37), channel_id=1, source_target_pairs={{0,16},{2,18},{4,20},{6,22},{8,24},{10,26},{12,28},{14,30},{16,0},... | collective-permute-start | bytes 248840 | tf_op jit(solution)/shard_map/ppermute | solution.py:154
  439.7 9.9 %collective-permute-start.78 = (bf16[2,64,576]{1,2,0:T(8,128)(2,1)}, bf16[2,64,576]{1,2,0:T(8,128)(2,1)}, u32[]{:S(2)}, u32[]{:S(2)}) collective-permute-start(bf16[2,64,576]{1,2,0:T(8,128)(2,1)} %dynamic-slice_bitcast_fusion.12), channel_id=1, source_target_pairs={{0,4},{2,6},{4,0},{6,2},{8,12},{10,14},{12,8},{14,10},{16,20},{18,... | collective-permute-start | bytes 442376 | tf_op jit(solution)/shard_map/ppermute | solution.py:154
  443.2 21.8 %collective-permute-start.73 = (bf16[2,2,96,576]{3,2,1,0:T(8,128)(2,1)}, bf16[2,2,96,576]{3,2,1,0:T(8,128)(2,1)}, u32[]{:S(2)}, u32[]{:S(2)}) collective-permute-start(bf16[2,2,96,576]{3,2,1,0:T(8,128)(2,1)} %bitcast.404), channel_id=1, source_target_pairs={{0,8},{2,10},{4,12},{6,14},{8,0},{10,2},{12,4},{14,6},{16,24},{18,... | collective-permute-start | bytes 1327112 | tf_op jit(solution)/shard_map/ppermute | solution.py:154
  450.7 7.5 %collective-permute-start.79 = (bf16[64,576]{0,1:T(8,128)(2,1)S(1)}, bf16[64,576]{0,1:T(8,128)(2,1)S(1)}, u32[]{:S(2)}, u32[]{:S(2)}) collective-permute-start(bf16[64,576]{0,1:T(8,128)(2,1)S(1)} %dynamic-slice_bitcast_fusion.28), channel_id=1, source_target_pairs={{0,16},{2,18},{4,20},{6,22},{8,24},{10,26},{12,28},{14,30},{16,0},... | collective-permute-start | bytes 221192 | tf_op jit(solution)/shard_map/ppermute | solution.py:154
  452.9 11.5 %collective-permute-start.31 = (bf16[2,32,1728]{2,1,0:T(8,128)(2,1)S(1)}, bf16[2,32,1728]{2,1,0:T(8,128)(2,1)S(1)}, u32[]{:S(2)}, u32[]{:S(2)}) collective-permute-start(bf16[2,32,1728]{2,1,0:T(8,128)(2,1)S(1)} %dynamic-slice_bitcast_fusion.24), channel_id=1, source_target_pairs={{0,8},{2,10},{4,12},{6,14},{8,0},{10,2},{12,4},{14,6},{16,24},{18,... | collective-permute-start | bytes 663560 | tf_op jit(solution)/shard_map/ppermute | solution.py:154
  460.7 14.5 %collective-permute-start.69 = (bf16[2,2,128,576]{2,3,1,0:T(8,128)(2,1)}, bf16[2,2,128,576]{2,3,1,0:T(8,128)(2,1)}, u32[]{:S(2)}, u32[]{:S(2)}) collective-permute-start(bf16[2,2,128,576]{2,3,1,0:T(8,128)(2,1)} %dynamic-slice_bitcast_fusion.5), channel_id=1, source_target_pairs={{0,4},{2,6},{4,0},{6,2},{8,12},{10,14},{12,8},{14,10},{16,20},{18,... | collective-permute-start | bytes 1769480 | tf_op jit(solution)/shard_map/ppermute | solution.py:154
  465.1 8.3 %collective-permute-start.32 = (bf16[32,1728]{1,0:T(8,128)(2,1)}, bf16[32,1728]{1,0:T(8,128)(2,1)}, u32[]{:S(2)}, u32[]{:S(2)}) collective-permute-start(bf16[32,1728]{1,0:T(8,128)(2,1)} %dynamic-slice_bitcast_fusion.35), channel_id=1, source_target_pairs={{0,16},{2,18},{4,20},{6,22},{8,24},{10,26},{12,28},{14,30},{16,0},... | collective-permute-start | bytes 331784 | tf_op jit(solution)/shard_map/ppermute | solution.py:154
  466.6 9.9 %collective-permute-start.74 = (bf16[2,96,576]{1,2,0:T(8,128)(2,1)S(1)}, bf16[2,96,576]{1,2,0:T(8,128)(2,1)S(1)}, u32[]{:S(2)}, u32[]{:S(2)}) collective-permute-start(bf16[2,96,576]{1,2,0:T(8,128)(2,1)S(1)} %dynamic-slice_bitcast_fusion.13), channel_id=1, source_target_pairs={{0,2},{2,0},{4,6},{6,4},{8,10},{10,8},{12,14},{14,12},{16,18},{18,... | collective-permute-start | bytes 663560 | tf_op jit(solution)/shard_map/ppermute | solution.py:154
  476.4 8.4 %collective-permute-start.70 = (bf16[2,128,576]{1,2,0:T(8,128)(2,1)S(1)}, bf16[2,128,576]{1,2,0:T(8,128)(2,1)S(1)}, u32[]{:S(2)}, u32[]{:S(2)}) collective-permute-start(bf16[2,128,576]{1,2,0:T(8,128)(2,1)S(1)} %dynamic-slice_bitcast_fusion.14), channel_id=1, source_target_pairs={{0,8},{2,10},{4,12},{6,14},{8,0},{10,2},{12,4},{14,6},{16,24},{18,... | collective-permute-start | bytes 884744 | tf_op jit(solution)/shard_map/ppermute | solution.py:154
  476.7 8.4 %collective-permute-start.75 = (bf16[96,576]{0,1:T(8,128)(2,1)S(1)}, bf16[96,576]{0,1:T(8,128)(2,1)S(1)}, u32[]{:S(2)}, u32[]{:S(2)}) collective-permute-start(bf16[96,576]{0,1:T(8,128)(2,1)S(1)} %dynamic-slice_bitcast_fusion.29), channel_id=1, source_target_pairs={{0,16},{2,18},{4,20},{6,22},{8,24},{10,26},{12,28},{14,30},{16,0},... | collective-permute-start | bytes 331784 | tf_op jit(solution)/shard_map/ppermute | solution.py:154
  484.9 6.7 %collective-permute-start.71 = (bf16[128,576]{0,1:T(8,128)(2,1)S(1)}, bf16[128,576]{0,1:T(8,128)(2,1)S(1)}, u32[]{:S(2)}, u32[]{:S(2)}) collective-permute-start(bf16[128,576]{0,1:T(8,128)(2,1)S(1)} %dynamic-slice_bitcast_fusion.30), channel_id=1, source_target_pairs={{0,16},{2,18},{4,20},{6,22},{8,24},{10,26},{12,28},{14,30},{16,0},... | collective-permute-start | bytes 442376 | tf_op jit(solution)/shard_map/ppermute | solution.py:154
  (134 other events, 699.3 us)

commit v2 on v1

v2 whole, which is shorter than its diff:
```python
import functools
import math

import jax
import jax.numpy as jnp
from jax import lax
from jax.experimental import pallas as pl
from jax.experimental.pallas import tpu as pltpu
from jax.sharding import PartitionSpec as P

HEADS = 16
EPS = 1e-06
MASKED = -1e30
F32 = jnp.float32
BF16 = jnp.bfloat16
GELU_A = math.sqrt(2.0 / math.pi)
GELU_B = 0.044715
NEAR, FAR = 0, 1
COST = 1000


def product(left, right):
    return jnp.dot(left, right, preferred_element_type=F32)


def transpose_product(left, right):
    return lax.dot_general(left, right, (((0,), (0,)), ((), ())), preferred_element_type=F32)


def product_back(left, right):
    return lax.dot_general(left, right, (((1,), (1,)), ((), ())), preferred_element_type=F32)


def swap(values_in):
    return lax.ppermute(values_in, "blk", [(0, 1), (1, 0)])


def pick(values_in, index, axis=0):
    return lax.dynamic_index_in_dim(values_in, index, axis, keepdims=False)


def columns_of(values_in, index, length):
    return lax.dynamic_slice_in_dim(values_in, index * length, length, 1)


def in_order(core, mine, theirs, axis=0):
    first = jnp.where(core == 0, mine, theirs)
    second = jnp.where(core == 0, theirs, mine)
    return jnp.concatenate([first, second], axis)


def after(values_in, token):
    return lax.optimization_barrier((values_in, token))[0]


def call(kernel, outs, ins, scratch=(), name=None, prefetch=(), limit=24):
    specs, arrays = [], []
    for item in prefetch:
        specs.append(pl.BlockSpec(memory_space=pltpu.SMEM))
        arrays.append(item)
    place = lambda item: pl.BlockSpec(memory_space=pltpu.HBM if isinstance(item, tuple) else pltpu.VMEM)
    plain = lambda item: item[0] if isinstance(item, tuple) else item
    return pl.pallas_call(
        kernel,
        out_shape=tuple(plain(out) for out in outs),
        in_specs=specs + [place(item) for item in ins],
        out_specs=tuple(place(out) for out in outs),
        scratch_shapes=list(scratch),
        compiler_params=pltpu.CompilerParams(vmem_limit_bytes=limit * 1024 * 1024),
        cost_estimate=pl.CostEstimate(flops=COST, bytes_accessed=10**6, transcendentals=0),
        name=name,
    )(*arrays, *[plain(item) for item in ins])


class Outgoing:
    def __init__(self, sems):
        self.sems, self.copies = sems, []

    def start(self, source, target):
        copy = pltpu.make_async_copy(source, target, self.sems.at[len(self.copies)])
        copy.start()
        self.copies.append(copy)

    def wait(self):
        for copy in self.copies:
            copy.wait()


def shape_f32(*dims):
    return jax.ShapeDtypeStruct(dims, F32)


def shape_bf16(*dims):
    return jax.ShapeDtypeStruct(dims, BF16)


def row_mean(values_in):
    return jnp.mean(values_in, -1, keepdims=True)


def normalize(values_in):
    centred = values_in - row_mean(values_in)
    inverse = lax.rsqrt(row_mean(centred * centred) + EPS)
    return centred * inverse, inverse


def normalize_back(normed, inverse, grad):
    return inverse * (grad - row_mean(grad) - normed * row_mean(grad * normed))


def head_window(head, size):
    low, high = head * size, (head + 1) * size
    start, stop = low // 128 * 128, -(-high // 128) * 128
    lane = lax.broadcasted_iota(jnp.int32, (1, stop - start), 1) + start
    return slice(start, stop), (lane >= low) & (lane < high)


def valid_slots(ids_ref, rows, dimension):
    strip = rows // 2
    shape = (1, rows) if dimension == 1 else (rows, 1)
    near = lax.broadcasted_iota(jnp.int32, shape, dimension)
    core = ids_ref[0]
    position = jnp.where(near < strip, core * strip + near, (1 - core) * strip + near - strip)
    return position < ids_ref[1]


def start_rows(core, mine, theirs, target, sems, at):
    rows = mine.shape[0]
    copies = (
        pltpu.make_async_copy(mine, target.at[pl.ds(pl.multiple_of(core * rows, 64), rows)], sems.at[at]),
        pltpu.make_async_copy(
            theirs, target.at[pl.ds(pl.multiple_of((1 - core) * rows, 64), rows)], sems.at[at + 1]
        ),
    )
    for copy in copies:
        copy.start()
    return copies


def pieces_of(mod_ref, width):
    return [mod_ref[:, index * width : (index + 1) * width] for index in range(6)]


def front_kernel(
    ids_ref,
    mine_ref,
    theirs_ref,
    mod_ref,
    wq_mine,
    wq_theirs,
    wp_mine,
    wp_theirs,
    qv_bias_ref,
    proj_bias_ref,
    both_out,
    q_out,
    k_out,
    v_out,
    log_out,
    attn_out,
    h_mlp_ref,
    wq_ref,
    wp_ref,
    both_ref,
    q_ref,
    k_ref,
    v_ref,
    log_ref,
    attn_ref,
    sems,
    out_sems,
):
    out = Outgoing(out_sems)
    core = ids_ref[0]
    q_copies = start_rows(core, wq_mine, wq_theirs, wq_ref, sems, 0)
    p_copies = start_rows(core, wp_mine, wp_theirs, wp_ref, sems, 2)
    rows, width = q_ref.shape
    size = width // HEADS
    shift_attn, scale_attn, gate_attn, shift_mlp, scale_mlp, _ = pieces_of(mod_ref, width)
    tokens = jnp.concatenate([mine_ref[...], theirs_ref[...]], 0).astype(F32)
    normed, _ = normalize(tokens)
    h_attn = (normed * (1.0 + scale_attn) + shift_attn).astype(BF16)
    both_ref[0] = h_attn
    out.start(both_ref.at[0], both_out.at[0])
    for copy in q_copies:
        copy.wait()
    q_ref[...] = (product(h_attn, wq_ref[:, :width]) + qv_bias_ref[:, :width].astype(F32)).astype(BF16)
    k_ref[...] = product(h_attn, wq_ref[:, width : 2 * width]).astype(BF16)
    v_ref[...] = (
        product(h_attn, wq_ref[:, 2 * width :]) + qv_bias_ref[:, width:].astype(F32)
    ).astype(BF16)

    for source, target in ((q_ref, q_out), (k_ref, k_out), (v_ref, v_out)):
        out.start(source, target)

    valid = valid_slots(ids_ref, rows, 1)
    lane = lax.broadcasted_iota(jnp.int32, (1, 128), 1)
    logs = jnp.zeros((rows, 128), F32)
    for head in range(HEADS):
        columns, own = head_window(head, size)
        query = jnp.where(own, q_ref[:, columns].astype(F32), 0.0).astype(BF16)
        scores = jnp.where(valid, product_back(query, k_ref[:, columns]) * size ** (-0.5), MASKED)
        largest = jnp.max(scores, -1, keepdims=True)
        exponent = jnp.exp(scores - largest)
        totals = jnp.sum(exponent, -1, keepdims=True)
        probs = (exponent / totals).astype(BF16)
        attended = product(probs, v_ref[:, columns])
        before = both_ref[1, :, columns].astype(F32)
        both_ref[1, :, columns] = jnp.where(own, attended, before).astype(BF16)
        logs = jnp.where(lane == head, largest + jnp.log(totals), logs)
    log_ref[...] = logs
    out.start(log_ref, log_out)
    out.start(both_ref.at[1], both_out.at[1])

    for copy in p_copies:
        copy.wait()
    attn = product(both_ref[1], wp_ref[...]) + proj_bias_ref[...].astype(F32)
    attn_ref[...] = attn
    out.start(attn_ref, attn_out)
    normed_mlp, _ = normalize(tokens + gate_attn * attn)
    h_mlp_ref[...] = (normed_mlp * (1.0 + scale_mlp) + shift_mlp).astype(BF16)
    out.wait()


def bits_in_order(kind, core):
    return (core, 1 - core, 2, 3) if kind == NEAR else (2, core, 1 - core, 3)


def store_halves(read, kind, ids_ref, keep_ref, send_ref, columns=slice(None), high=None):
    core = ids_ref[0]
    order = bits_in_order(kind, core)
    mine = ids_ref[2 + order[0]]
    for index in range(8 if high is None else 4):
        if high is None:
            slot = index
            base = ((index >> 2) << order[1]) + (((index >> 1) & 1) << order[2]) + ((index & 1) << order[3])
        else:
            slot = (index, high)
            base = ((index >> 1) << order[1]) + ((index & 1) << order[2])
        for target, value in ((keep_ref, mine), (send_ref, 1 - mine)):
            block = base + (value << order[0])
            where = slot if isinstance(slot, tuple) else (slot,)
            target[(*where, slice(None), columns)] = read(block).astype(BF16)


def rows_of(total_ref, stride, first, count):
    return lambda block: total_ref[pl.ds(pl.multiple_of(block * stride + first, 8), count), :]


def start_hidden_weights(core, w1_mine, w1_theirs, w2, w1_ref, w2_ref, sems, chunks):
    half = w1_theirs.shape[1]
    length = half // chunks
    copies = []
    for chunk in range(chunks):
        here = pl.ds(chunk * length, length)
        mine = w1_mine.at[:, pl.ds(pl.multiple_of(core * half + chunk * length, 128), length)]
        second = pltpu.make_async_copy(w2.at[here], w2_ref.at[here], sems.at[3 * chunk + 2])
        second.start()
        first = start_rows(core, mine, w1_theirs.at[:, here], w1_ref.at[:, here], sems, 3 * chunk)
        copies.append((second, *first))
    return copies


def hidden_kernel(
    ids_ref,
    h_own_ref,
    h_other_ref,
    gm_own_ref,
    gm_other_ref,
    w1_mine,
    w1_theirs,
    w2,
    bias_ref,
    act_ref,
    gp_ref,
    bias_grad_ref,
    *rest,
):
    core = ids_ref[0]
    w1_ref, w2_ref, total_ref, sems = rest[-4:]
    if len(rest) > 4:
        keep_out, send_out, keep_ref, send_ref, out_sems = rest[:5]
        out = Outgoing(out_sems)
    length, half = total_ref.shape[1], act_ref.shape[1]
    copies = start_hidden_weights(core, w1_mine, w1_theirs, w2, w1_ref, w2_ref, sems, half // length)
    h_all = jnp.concatenate([h_own_ref[...], h_other_ref[...]], 0)
    gm_all = jnp.concatenate([gm_own_ref[...], gm_other_ref[...]], 0)
    for chunk in range(half // length):
        for copy in copies[chunk]:
            copy.wait()
        here = slice(chunk * length, (chunk + 1) * length)
        bias = bias_ref[:, pl.ds(pl.multiple_of(core * half + chunk * length, 128), length)].astype(F32)
        grad_act = product_back(gm_all, w2_ref[here, :])
        value = product(h_all, w1_ref[:, here]) + bias
        square = value * value
        tanh = jnp.tanh(GELU_A * value * (1.0 + GELU_B * square))
        half_up = 0.5 * (1.0 + tanh)
        act_ref[:, here] = (value * half_up).astype(BF16)
        slope = half_up + 0.5 * value * (1.0 - tanh * tanh) * (GELU_A * (1.0 + 3.0 * GELU_B * square))
        grad_pre = (grad_act * slope).astype(BF16)
        gp_ref[:, here] = grad_pre
        bias_grad_ref[:, here] = jnp.sum(grad_pre.astype(F32), 0, keepdims=True)
        if len(rest) > 4:
            total_ref[...] = transpose_product(h_all, grad_pre)
            rows = keep_ref.shape[2]
            read = rows_of(total_ref, rows, 0, rows)
            store_halves(read, NEAR, ids_ref, keep_ref.at[chunk], send_ref.at[chunk])
            out.start(send_ref.at[chunk], send_out.at[:, :, here])
            out.start(keep_ref.at[chunk], keep_out.at[:, :, here])
    if len(rest) > 4:
        out.wait()


def fc2_grad_kernel(ids_ref, gm_own_ref, gm_other_ref, *rest):
    act_ref, got_ref, targets, outs = rest[0], rest[1], rest[2:6], rest[6:10]
    columns_ref, turned_ref, total_ref, out_sems = rest[10:]
    out = Outgoing(out_sems)
    core = ids_ref[0]
    rows, part = gm_own_ref.shape[0], columns_ref.shape[1]
    for index in range(2):

        @pl.when(core == index)
        def _():
            own = gm_own_ref[:, index * part : (index + 1) * part]
            other = gm_other_ref[:, index * part : (index + 1) * part]
            columns_ref[:rows] = own
            columns_ref[rows:] = other
            turned_ref[:rows] = other
            turned_ref[rows:] = own

    near, far = outs[0].shape[2], outs[2].shape[2]
    half_block = near + far
    length = act_ref.shape[1] // 3
    for side, (ref, grads) in enumerate(((act_ref, columns_ref), (got_ref, turned_ref))):
        for start in range(0, 3 * length, length):
            here = slice(start, start + length)
            total_ref[here, :] = transpose_product(ref[:, here], grads[...])
        high = core if side == 0 else 1 - core
        for kind, (first, count) in enumerate(((0, near), (near, far))):
            for place in range(2):
                store_halves(
                    rows_of(total_ref, 2 * half_block, place * half_block + first, count),
                    kind,
                    ids_ref,
                    outs[2 * kind],
                    outs[2 * kind + 1],
                    slice(place * part, (place + 1) * part),
                    high,
                )
            for index in (2 * kind + 1, 2 * kind):
                out.start(outs[index].at[:, high], targets[index].at[:, high])
    out.wait()


def advance_kernel(ids_ref, keep_there, got_there, keep_here, got_here, send_ref, next_ref):
    send_ref[...] = (keep_there[...].astype(F32) + got_there[...].astype(F32)).astype(BF16)
    next_ref[...] = (keep_here[...].astype(F32) + got_here[...].astype(F32)).astype(BF16)


def advance_call(ids, keep, got, kind, step):
    count, rows, columns = keep.shape[0] // 2, *keep.shape[1:]

    def half(there):
        def index_map(index, ids_ref):
            mine = ids_ref[2 + bits_in_order(kind, ids_ref[0])[step]]
            return ((1 - mine if there else mine) * count + index, 0, 0)

        return pl.BlockSpec((1, rows, columns), index_map)

    out = pl.BlockSpec((1, rows, columns), lambda index, ids_ref: (index, 0, 0))
    shape = shape_bf16(count, rows, columns)
    return pl.pallas_call(
        advance_kernel,
        out_shape=(shape, shape),
        grid_spec=pltpu.PrefetchScalarGridSpec(
            num_scalar_prefetch=1,
            grid=(count,),
            in_specs=[half(True), half(True), half(False), half(False)],
            out_specs=(out, out),
        ),
        compiler_params=pltpu.CompilerParams(vmem_limit_bytes=16 * 1024 * 1024),
        cost_estimate=pl.CostEstimate(flops=COST, bytes_accessed=10**6, transcendentals=0),
        name="advance",
    )(ids, keep, got, keep, got)


def partial_kernel(
    ids_ref, act_ref, gp_ref, w1_mine, w1_theirs, w2, own_ref, their_ref, w1_ref, w2_ref, sems
):
    core = ids_ref[0]
    half = act_ref.shape[1]
    rows, width = own_ref.shape[1:]
    length = width // 3
    seconds = []
    for chunk in range(3):
        here = pl.ds(chunk * length, length)
        seconds.append(pltpu.make_async_copy(w2.at[:, here], w2_ref.at[:, here], sems.at[2 + chunk]))
        seconds[-1].start()
    mine = w1_mine.at[:, pl.ds(pl.multiple_of(core * half, 128), half)]
    firsts = start_rows(core, mine, w1_theirs, w1_ref, sems, 0)
    for index in range(2):
        for chunk in range(3):
            here = slice(chunk * length, (chunk + 1) * length)
            if index == 0:
                seconds[chunk].wait()
                value = product(act_ref[...], w2_ref[:, here])
            else:
                if chunk == 0:
                    for copy in firsts:
                        copy.wait()
                value = product_back(gp_ref[...], w1_ref[here, :])
            own_ref[index, :, here] = value[:rows]
            their_ref[index, :, here] = value[rows:]


def middle_back_kernel(
    ids_ref,
    mine_ref,
    theirs_ref,
    cot_mine_ref,
    cot_theirs_ref,
    mod_ref,
    attn_ref,
    part_ref,
    got_ref,
    wp_mine,
    wp_theirs,
    q_ref,
    k_ref,
    v_ref,
    log_ref,
    grad_middle_out,
    gq_out,
    gk_out,
    gv_out,
    g_mine_ref,
    g_send_ref,
    sums_ref,
    wp_ref,
    ga_ref,
    grad_middle_ref,
    gq_ref,
    gk_ref,
    gv_ref,
    sems,
    out_sems,
):
    out = Outgoing(out_sems)
    core = ids_ref[0]
    copies = start_rows(core, wp_mine, wp_theirs, wp_ref, sems, 0)
    rows, width = q_ref.shape
    size, part = width // HEADS, width // 2
    _, _, gate_attn, _, scale_mlp, _ = pieces_of(mod_ref, width)
    tokens = jnp.concatenate([mine_ref[...], theirs_ref[...]], 0).astype(F32)
    cot = jnp.concatenate([cot_mine_ref[...], cot_theirs_ref[...]], 0).astype(F32)
    grad_out = jnp.where(valid_slots(ids_ref, rows, 0), cot, 0.0)
    grad_h = part_ref[1] + got_ref[1]
    attn = attn_ref[...]
    normed, inverse = normalize(tokens + gate_attn * attn)
    grad_middle = grad_out + normalize_back(normed, inverse, grad_h * (1.0 + scale_mlp))
    grad_middle_ref[...] = grad_middle
    out.start(grad_middle_ref, grad_middle_out)
    grad_attn = (gate_attn * grad_middle).astype(BF16)
    column_sum = lambda array: jnp.sum(array, 0, keepdims=True)
    sums_ref[0:1] = column_sum(grad_middle * attn)
    sums_ref[1:2] = column_sum(grad_h)
    sums_ref[2:3] = column_sum(grad_h * normed)
    sums_ref[3:4] = column_sum(grad_attn.astype(F32))
    for copy in copies:
        copy.wait()
    ga_ref[...] = product_back(grad_attn, wp_ref[...]).astype(BF16)

    valid = valid_slots(ids_ref, rows, 1)
    scale = size ** (-0.5)
    for head in range(HEADS):
        columns, own = head_window(head, size)
        query = q_ref[:, columns]
        key = k_ref[:, columns]
        grad = ga_ref[:, columns]
        own_query = jnp.where(own, query.astype(F32), 0.0).astype(BF16)
        own_grad = jnp.where(own, grad.astype(F32), 0.0).astype(BF16)
        scores = jnp.where(valid, product_back(own_query, key) * scale, MASKED)
        probs = jnp.exp(scores - log_ref[:, head : head + 1])
        grad_probs = product_back(own_grad, v_ref[:, columns])
        inner = jnp.sum(probs * grad_probs, -1, keepdims=True)
        grad_scores = (probs * (grad_probs - inner)).astype(BF16)
        grad_query = product(grad_scores, key) * scale
        grad_key = transpose_product(grad_scores, query) * scale
        grad_value = transpose_product(probs.astype(BF16), grad)
        gq_ref[:, columns] = jnp.where(own, grad_query, gq_ref[:, columns].astype(F32)).astype(BF16)
        gk_ref[:, columns] = jnp.where(own, grad_key, gk_ref[:, columns].astype(F32)).astype(BF16)
        gv_ref[:, columns] = jnp.where(own, grad_value, gv_ref[:, columns].astype(F32)).astype(BF16)
    for source, target in ((gq_ref, gq_out), (gk_ref, gk_out), (gv_ref, gv_out)):
        out.start(source, target)
    sums_ref[4:5] = column_sum(gq_ref[...].astype(F32))
    sums_ref[5:6] = column_sum(gv_ref[...].astype(F32))

    @pl.when(core == 0)
    def _():
        fill_half(0, g_mine_ref, grad_attn, gq_ref, gk_ref, gv_ref, width, part)
        fill_half(1, g_send_ref, grad_attn, gq_ref, gk_ref, gv_ref, width, part)

    @pl.when(core == 1)
    def _():
        fill_half(1, g_mine_ref, grad_attn, gq_ref, gk_ref, gv_ref, width, part)
        fill_half(0, g_send_ref, grad_attn, gq_ref, gk_ref, gv_ref, width, part)
    out.wait()


def fill_half(index, fill, grad_attn, gq_ref, gk_ref, gv_ref, width, part):
    if index == 0:
        fill[:, :width] = gq_ref[...]
        fill[:, width : width + part] = gk_ref[:, :part]
    else:
        fill[:, :part] = gk_ref[:, part:]
        fill[:, part : part + width] = gv_ref[...]
    fill[:, width + part :] = grad_attn[:, index * part : (index + 1) * part]


def qkv_grad_kernel(ids_ref, g_mine_ref, g_got_ref, both_ref, both_got_ref, *rest):
    targets, outs, total_ref, out_sems = rest[:4], rest[4:8], rest[8], rest[9]
    out = Outgoing(out_sems)
    width = both_ref.shape[2]
    grads = jnp.concatenate([g_mine_ref[...], g_got_ref[...]], 0)
    h_attn = jnp.concatenate([both_ref[0], both_got_ref[0]], 0)
    attended = jnp.concatenate([both_ref[1], both_got_ref[1]], 0)
    wide = 3 * width // 2
    rows, length = outs[0].shape[1], total_ref.shape[1]
    for chunk in (2, 0, 1):
        start = chunk * length
        if start + length <= wide:
            total_ref[...] = transpose_product(h_attn, grads[:, start : start + length])
            kind, columns = NEAR, slice(start, start + length)
        else:
            cut_at = wide - start
            total_ref[:, :cut_at] = transpose_product(h_attn, grads[:, start:wide])
            total_ref[:, cut_at:] = transpose_product(attended, grads[:, wide:])
            kind, columns = FAR, slice(0, length)
        store_halves(
            rows_of(total_ref, rows, 0, rows), kind, ids_ref, outs[2 * kind], outs[2 * kind + 1], columns
        )
        for index in (2 * kind + 1, 2 * kind):
            out.start(outs[index].at[:, :, columns], targets[index].at[:, :, columns])
    out.wait()


def last_kernel(
    ids_ref,
    mine_ref,
    theirs_ref,
    cot_mine_ref,
    cot_theirs_ref,
    mod_ref,
    attn_ref,
    part_ref,
    got_ref,
    fc2_bias_ref,
    wq_mine,
    wq_theirs,
    gq_ref,
    gk_ref,
    gv_ref,
    grad_middle_ref,
    sums_ref,
    result_ref,
    input_grad_ref,
    mod_grad_ref,
    wq_ref,
    sems,
):
    core = ids_ref[0]
    copies = start_rows(core, wq_mine, wq_theirs, wq_ref, sems, 0)
    rows, width = gq_ref.shape
    _, scale_attn, gate_attn, _, _, gate_mlp = pieces_of(mod_ref, width)
    tokens = jnp.concatenate([mine_ref[...], theirs_ref[...]], 0).astype(F32)
    cot = jnp.concatenate([cot_mine_ref[...], cot_theirs_ref[...]], 0).astype(F32)
    valid = valid_slots(ids_ref, rows, 0)
    mlp = part_ref[0] + got_ref[0] + fc2_bias_ref[...].astype(F32)
    middle = tokens + gate_attn * attn_ref[...]
    result_ref[...] = jnp.where(valid, middle + gate_mlp * mlp, 0.0).astype(BF16)
    column_sum = lambda array: jnp.sum(array, 0, keepdims=True)
    gate_mlp_sum = column_sum(jnp.where(valid, cot, 0.0) * mlp)
    normed, inverse = normalize(tokens)
    for copy in copies:
        copy.wait()
    grad_h = product_back(gq_ref[...], wq_ref[:, :width])
    grad_h += product_back(gk_ref[...], wq_ref[:, width : 2 * width])
    grad_h += product_back(gv_ref[...], wq_ref[:, 2 * width :])
    input_grad_ref[...] = grad_middle_ref[...] + normalize_back(
        normed, inverse, grad_h * (1.0 + scale_attn)
    )
    parts = (
        column_sum(grad_h),
        column_sum(grad_h * normed),
        sums_ref[0:1],
        sums_ref[1:2],
        sums_ref[2:3],
        gate_mlp_sum,
    )
    for index, value in enumerate(parts):
        mod_grad_ref[:, index * width : (index + 1) * width] = value


def partners(bit, count):
    return [(index, index ^ (1 << bit)) for index in range(count)]


def reduce_chunk(values_in, order, count):
    bits = count.bit_length() - 1
    place = lax.axis_index("dp")
    left = list(range(bits - 1, -1, -1))
    current = values_in.reshape((2,) * bits + values_in.shape[1:])
    for step, bit in enumerate(order):
        mine = (place >> bit) & 1
        axis = left.index(bit)
        send = pick(current, 1 - mine, axis).astype(BF16)
        keep = pick(current, mine, axis)
        left.pop(axis)
        got = lax.ppermute(send, "dp", partners(bit, count))
        current = keep.astype(F32) + got.astype(F32)
        if step < bits - 1:
            current = current.astype(BF16)
    return current


def reduce_scatter(values_in):
    count = lax.axis_size("dp")
    rows = values_in.shape[0] // count
    blocks = values_in.reshape(count, rows, values_in.shape[1])
    return reduce_chunk(blocks, range(count.bit_length() - 1), count)


class Flow:
    def __init__(self, ids, kind, keep, send):
        self.ids, self.kind, self.step = ids, kind, 0
        self.keep = keep
        self.send(send)

    def send(self, array):
        pairs = []
        for core in range(2):
            bit = bits_in_order(self.kind, core)[self.step]
            pairs += [(2 * place + core, 2 * (place ^ (1 << bit)) + core) for place in range(16)]
        self.got = lax.ppermute(array, ("dp", "blk"), pairs)

    def advance(self, token):
        got = after(self.got, token)
        self.step += 1
        if self.step == 4:
            self.total = (self.keep.astype(F32) + got.astype(F32))[0]
            return self.total
        send, self.keep = advance_call(self.ids, self.keep, got, self.kind, self.step)
        self.send(send)
        return send


class Gather:
    def __init__(self, array):
        self.array, self.bit, self.got = array, 0, None
        self.count = lax.axis_size("dp")
        self.send()

    def send(self):
        bits = self.count.bit_length() - 1
        self.got = lax.ppermute(self.array, "dp", partners(bits - 1 - self.bit, self.count))

    def advance(self, token):
        self.array = jnp.concatenate([self.array, after(self.got, token)], 0)
        self.bit += 1
        if 1 << self.bit < self.count:
            self.send()
        return self.array


def on_device(
    inputs,
    conditioning,
    grid_sizes,
    ada_weight,
    ada_bias,
    qkv_weight,
    qv_bias,
    proj_weight,
    proj_bias,
    fc1_weight,
    fc1_bias,
    fc2_weight,
    fc2_bias,
    cotangent,
):
    images, strip, width = inputs.shape
    data_count = lax.axis_size("dp")
    core = lax.axis_index("blk")
    other = 1 - core
    place = lax.axis_index("dp")
    part = ada_weight.shape[0]
    hidden = fc1_weight.shape[1]
    half_hidden = hidden // 2
    rows = images * strip
    split = data_count == 16
    area = pick(grid_sizes[:, 0] * grid_sizes[:, 1], core)
    ids = jnp.stack([core, area] + [(place >> bit) & 1 for bit in range(4)]).astype(jnp.int32)

    pair = jnp.stack([pick(inputs, other), pick(cotangent, other)])
    pair = swap(pair)
    mine_inputs, their_inputs = pick(inputs, core), pair[0]
    mine_cot, their_cot = pick(cotangent, core), pair[1]
    qkv_theirs = swap(qkv_weight)
    proj_theirs = swap(proj_weight)
    fc1_theirs = swap(columns_of(fc1_weight, other, half_hidden))

    cond_f32 = conditioning.astype(F32)
    silu_cond, silu_back = jax.vjp(jax.nn.silu, cond_f32)
    silu_low = silu_cond.astype(BF16)
    modulation_part = product(columns_of(silu_low, core, part), ada_weight)
    modulation = modulation_part + swap(modulation_part) + ada_bias.astype(F32)
    own_modulation = pick(modulation, core)[None, :]
    gate_mlp = own_modulation[:, 5 * width :]

    near = jnp.arange(strip, dtype=jnp.int32)
    valid = (jnp.concatenate([core * strip + near, other * strip + near]) < area)[:, None]
    cot = jnp.concatenate([mine_cot, their_cot], 0).astype(F32)
    grad_mlp = (gate_mlp * jnp.where(valid, cot, 0.0)).astype(BF16)
    grad_mlp_other = swap(grad_mlp)

    square = shape_bf16(rows, width)
    sems = lambda count: pltpu.SemaphoreType.DMA((count,))
    outs = [shape_bf16(2, rows, width), square, square, square, shape_f32(rows, 128), shape_f32(rows, width)]
    buffers = lambda shapes: [pltpu.VMEM(shape.shape, shape.dtype) for shape in shapes]
    both, query, key, value, logs, attn, h_mlp = call(
        front_kernel,
        [(out, "hbm") for out in outs] + [square],
        (
            after(mine_inputs, grad_mlp_other),
            their_inputs,
            own_modulation,
            (qkv_weight, "hbm"),
            (qkv_theirs, "hbm"),
            (proj_weight, "hbm"),
            (proj_theirs, "hbm"),
            qv_bias[None, :],
            proj_bias[None, :],
        ),
        [pltpu.VMEM((width, 3 * width), BF16), pltpu.VMEM((width, width), BF16)] + buffers(outs) + [sems(4), sems(7)],
        name="front",
        prefetch=(ids,),
    )
    h_mlp_other = swap(h_mlp)
    both_got = swap(after(both, h_mlp_other))

    length = half_hidden // 3
    block = width // 16
    weights = ((fc1_weight, "hbm"), (fc1_theirs, "hbm"), (fc2_weight, "hbm"))
    room = [pltpu.VMEM((width, half_hidden), BF16), pltpu.VMEM((half_hidden, width), BF16)]
    wide = shape_bf16(2 * rows, half_hidden)
    flowing = [(shape_bf16(8, block, half_hidden), "hbm")] * 2 if split else []
    staged = [pltpu.VMEM((3, 8, block, length), BF16)] * 2 + [sems(6)] if split else []
    results = call(
        hidden_kernel,
        [wide, wide, shape_f32(1, half_hidden)] + flowing,
        (h_mlp, h_mlp_other, grad_mlp, grad_mlp_other, *weights, fc1_bias[None, :]),
        staged + room + [pltpu.VMEM((width, length), F32), sems(9)],
        name="hidden",
        prefetch=(ids,),
        limit=32,
    )
    act, grad_pre, fc1_bias_part = results[:3]
    act_got = swap(act)
    if split:
        fc1_flow = Flow(ids, NEAR, *results[3:])
    pair_f32 = shape_f32(2, rows, width)
    own_part, their_part = call(
        partial_kernel,
        (pair_f32, pair_f32),
        (after(act, both_got), grad_pre, *weights),
        room + [sems(5)],
        name="partial",
        prefetch=(ids,),
        limit=32,
    )
    got_part = swap(their_part)
    token = their_part
    if split:
        stripes = hidden // 16 // 6
        near, far = shape_bf16(4, 2, stripes, width), shape_bf16(4, 2, 2 * stripes, width)
        outs = [near, near, far, far]
        results = call(
            fc2_grad_kernel,
            [(out, "hbm") for out in outs],
            (after(grad_mlp, token), grad_mlp_other, act, act_got),
            buffers(outs)
            + [pltpu.VMEM((2 * rows, part), BF16)] * 2
            + [pltpu.VMEM((half_hidden, part), F32), sems(8)],
            name="fc2_grad",
            prefetch=(ids,),
        )
        results = [array.reshape(8, *array.shape[2:]) for array in results]
        fc2_near, fc2_far = Flow(ids, NEAR, *results[:2]), Flow(ids, FAR, *results[2:])
        token = results[1]

    pads = shape_bf16(rows, 4 * part)
    outs = [shape_f32(rows, width), square, square, square]
    grad_middle, grad_query, grad_key, grad_value, g_mine, g_send, sums = call(
        middle_back_kernel,
        [(out, "hbm") for out in outs] + [pads, pads, shape_f32(8, width)],
        (
            mine_inputs,
            their_inputs,
            mine_cot,
            their_cot,
            own_modulation,
            attn,
            after(own_part, token),
            got_part,
            (proj_weight, "hbm"),
            (proj_theirs, "hbm"),
            query,
            key,
            value,
            logs,
        ),
        [pltpu.VMEM((width, width), BF16), pltpu.VMEM((rows, width), BF16)] + buffers(outs) + [sems(2), sems(4)],
        name="middle_back",
        prefetch=(ids,),
    )
    g_got = swap(g_send)
    token = g_send
    if split:
        token = fc1_flow.advance(token)
        near, far = shape_bf16(8, block, 2 * length), shape_bf16(8, block, length)
        outs = [near, near, far, far]
        results = call(
            qkv_grad_kernel,
            [(out, "hbm") for out in outs],
            (after(g_mine, token), g_got, both, both_got),
            buffers(outs) + [pltpu.VMEM((width, length), F32), sems(6)],
            name="qkv_grad",
            prefetch=(ids,),
        )
        qkv_near, qkv_far = Flow(ids, NEAR, *results[:2]), Flow(ids, FAR, *results[2:])
        token = fc2_near.advance(results[1])

    result, input_grad, mod_sums = call(
        last_kernel,
        (square, shape_f32(rows, width), shape_f32(1, 6 * width)),
        (
            mine_inputs,
            their_inputs,
            mine_cot,
            their_cot,
            own_modulation,
            attn,
            own_part,
            got_part,
            fc2_bias[None, :],
            (qkv_weight, "hbm"),
            (qkv_theirs, "hbm"),
            after(grad_query, token),
            grad_key,
            grad_value,
            grad_middle,
            sums,
        ),
        (pltpu.VMEM((width, 3 * width), BF16), sems(2)),
        name="last",
        prefetch=(ids,),
    )
    def advance(token, *flows):
        for flow in flows:
            token = flow.advance(token)
        return token

    token = mod_sums
    if split:
        token = advance(token, fc2_far, fc1_flow)

    together = lambda array, axis: lax.all_gather(array, "blk", axis=axis, tiled=True)
    modulation_low = together(after(mod_sums, token).astype(BF16), 0)
    silu_grad = together(product_back(modulation_low, ada_weight), 1)
    cond_grad = silu_back(silu_grad)[0]
    by_device = lambda array: array.reshape(data_count, -1)
    image_bias = jnp.concatenate(
        [by_device(sums[4:6]), by_device(sums[3]), by_device(jnp.sum(after(grad_mlp, token).astype(F32), 0))], 1
    )
    small = jnp.concatenate(
        [
            silu_low,
            columns_of(modulation_low, core, 3 * width),
            image_bias.astype(BF16).reshape(images, -1),
            fc1_bias_part.astype(BF16).reshape(images, -1),
        ],
        1,
    )
    gather = Gather(small)
    back = lambda array: in_order(core, array[None, :strip], swap(array[None, strip:]))
    if split:
        token = advance(small, qkv_near, qkv_far, gather)
        output = back(after(result, token))
        token = advance(token, fc2_near, fc2_far, gather)
        input_grad = back(after(input_grad, token))
        token = advance(token, fc1_flow, qkv_near, qkv_far, gather)
        token = advance(token, fc2_near, fc2_far, gather)
    else:
        output, input_grad = back(result), back(input_grad)
        while 1 << gather.bit < data_count:
            token = gather.advance(token)
    gathered = gather.array
    silu_rows = columns_of(gathered[:, :width], place, width // data_count)
    modulation_all = gathered[:, width : 4 * width]
    ada_grad = transpose_product(silu_rows, modulation_all)
    bias_all = gathered[:, 4 * width :].astype(F32)
    image_count = image_bias.size // images
    image_sums = jnp.sum(bias_all[:, :image_count].reshape(data_count, data_count, -1), 0)
    hidden_sums = jnp.sum(bias_all[:, image_count:].reshape(data_count, data_count // 2, -1), 0)
    ada_sums = jnp.sum(modulation_all.astype(F32), 0).reshape(data_count // 2, -1)
    near_half = jnp.where(place // (data_count // 2) == core, 1.0, 0.0)
    in_half = place % (data_count // 2)
    bias_sums = lax.psum(
        jnp.concatenate(
            [pick(ada_sums, in_half) * near_half, pick(image_sums, place), pick(hidden_sums, in_half) * near_half]
        ),
        "blk",
    )
    ends, at = [], 0
    for count in [6 * width, 2 * width, width, width]:
        at += count // data_count
        ends.append(at)
    ada_bias_grad, qv_bias_grad, proj_bias_grad, fc2_bias_grad, fc1_bias_grad = jnp.split(bias_sums, ends)
    biases = (ada_bias_grad, qv_bias_grad, proj_bias_grad, fc1_bias_grad, fc2_bias_grad)

    if split:
        token = advance(token, fc1_flow, qkv_near, qkv_far, fc2_near, fc2_far, qkv_near, qkv_far)
        fc1_grad = fc1_flow.total
        fc2_total = jnp.concatenate([fc2_near.total, fc2_far.total], 0)
        fc2_grad = jnp.concatenate([fc2_total[:, :part], fc2_total[:, part:]], 0)
        qkv_grad = jnp.concatenate([qkv_near.total, qkv_far.total[:, : 3 * part - 2 * length]], 1)
        proj_grad = qkv_far.total[:, 3 * part - 2 * length :]
    else:
        h_mlp_all = jnp.concatenate([h_mlp, h_mlp_other], 0)
        fc1_grad = reduce_scatter(transpose_product(h_mlp_all, grad_pre))
        grad_mlp_all = columns_of(jnp.concatenate([grad_mlp, grad_mlp_other], 0), core, part)
        turned = jnp.concatenate([grad_mlp_all[rows:], grad_mlp_all[:rows]], 0)
        fc2_term = in_order(
            core,
            transpose_product(act, grad_mlp_all).astype(BF16),
            transpose_product(act_got, turned).astype(BF16),
        )
        fc2_grad = reduce_scatter(fc2_term)
        g_all = jnp.concatenate([g_mine, g_got], 0)
        h_attn_all = jnp.concatenate([both[0], both_got[0]], 0)
        attended_all = jnp.concatenate([both[1], both_got[1]], 0)
        qkv_grad = reduce_scatter(transpose_product(h_attn_all, g_all[:, : 3 * part]))
        proj_grad = reduce_scatter(transpose_product(attended_all, g_all[:, 3 * part :]))
    return (
        output,
        input_grad,
        cond_grad,
        ada_grad,
        biases[0],
        qkv_grad,
        biases[1],
        proj_grad,
        biases[2],
        fc1_grad,
        biases[3],
        fc2_grad,
        biases[4],
    )


def solution(mesh):
    rows = P("dp", "blk", None)
    weight = P("blk", None)
    grads = (P("dp", "blk"), P("dp"))
    placed = (rows, P("dp", None), P("dp", None)) + (weight, P()) * 5 + (rows,)
    return jax.shard_map(
        on_device,
        mesh=mesh,
        in_specs=placed,
        out_specs=(rows, rows, P("dp", None)) + grads * 5,
        check_vma=False,
    )
```

time: 500 us -> 254 us (0.51)
  waiting for transfers between devices: 177 us -> 32 us
  Pallas kernels: 9.51 us -> 104 us
  local copies, waits for them, and re-layouts: 112 us -> 48.3 us
  matrix products: 61.3 us -> 12.1 us
  other arithmetic: 57.3 us -> 13.4 us
  starting transfers between devices: 72.9 us -> 31.9 us
  blocking collectives: 0 us -> 6.32 us
    ppermute x60 -> x24, waiting for transfers between devices: 175 us -> 25.2 us  [the longest x20 17.2 us: send(): self.got = lax.ppermute(array, ('dp', 'blk'), pairs)]
    pallas_call x2 -> x22, Pallas kernels: 9.51 us -> 104 us  [the longest x7 75.6 us: call(): pl.pallas_call(kernel, out_shape=tuple((plain(out) for out in outs)), in_...]
    ppermute x60 -> x24, starting transfers between devices: 68.2 us -> 29.1 us  [the longest x20 23.9 us: send(): self.got = lax.ppermute(array, ('dp', 'blk'), pairs)]
    convert_element_type x43 -> x3, other arithmetic: 22.1 us -> 1.28 us  [the longest x1 1.04 us: on_device(): bias_all = gathered[:, 4 * width:].astype(F32)]
    dynamic_slice x12 -> x2, local copies, waits for them, and re-layouts: 19.4 us -> 0.55 us  [pick(): return lax.dynamic_index_in_dim(values_in, index, axis, keepdims=False)]
    dot_general x5 -> x1, matrix products: 22.4 us -> 5.39 us  [product_back(): lax.dot_general(left, right, (((1,), (1,)), ((), ())), preferred_element_...]
    dot_general x5 -> x1, matrix products: 21 us -> 4.44 us  [product(): return jnp.dot(left, right, preferred_element_type=F32)]
    slice x18 -> x9, local copies, waits for them, and re-layouts: 18.6 us -> 2.27 us  [the longest x1 0.79 us: on_device(): proj_grad = qkv_far.total[:, 3 * part - 2 * length:]]
  transfers between devices with their start and end apart: 80 -> 37, of which waited for: 42 -> 11; matrix products, arithmetic and copies ran while one was open for 40% -> 17% of each run, Pallas kernels for 2% -> 42%
where the time goes in v2:
time: 254 us; the launch traced here: 250 us
  Pallas kernels  104 us (41%)
  local copies, waits for them, and re-layouts  48.3 us (19%)
  waiting for transfers between devices  32 us (13%)
  starting transfers between devices  31.9 us (13%)
  other arithmetic  13.4 us (5%)
  matrix products  12.1 us (5%)
  blocking collectives  6.32 us (2%)
    pallas_call x7, Pallas kernels, call(): pl.pallas_call(kernel, out_shape=tuple((plain(out) for out in outs)), in_...  75.6 us
    pallas_call x15, Pallas kernels, advance_call(): pl.pallas_call(advance_kernel, out_shape=(shape, shape), grid_spec=pltpu....  28.3 us
    unnamed x182, local copies, waits for them, and re-layouts  25.6 us
    ppermute x20, starting transfers between devices, send(): self.got = lax.ppermute(array, ('dp', 'blk'), pairs)  23.9 us
    ppermute x20, waiting for transfers between devices, send(): self.got = lax.ppermute(array, ('dp', 'blk'), pairs)  17.2 us
    ppermute x4, waiting for transfers between devices, send(): lax.ppermute(self.array, 'dp', partners(bits - 1 - self.bit, self.count))  8.02 us
    ppermute x13, waiting for transfers between devices, swap(): return lax.ppermute(values_in, 'blk', [(0, 1), (1, 0)])  6.8 us
    dot_general x1, matrix products, product_back(): lax.dot_general(left, right, (((1,), (1,)), ((), ())), preferred_element_...  5.39 us
  transfers between devices with their start and end apart: 37, of which 11 were waited for; matrix products, arithmetic and copies ran while one was open for 17% of the time, Pallas kernels for 42%

profile of v2, /device:TPU:0, one launch (start us, length us, event | category | flops | bytes accessed | tf_op | source)
XLA Modules:
  0.0 249.9 jit_solution(5325277862181673204)
XLA Ops:
  0.7 2.0 dynamic-slice_bitcast_fusion
  4.1 4.4 %fusion.15 = f32[2,6912]{1,0:T(2,128)S(1)} fusion(bf16[576,6912]{1,0:T(8,128)(2,1)} %param.17, bf16[2,1152]{1,0:T(2,128)(2,1)S(1)} %fusion.10, s32[]{:T(128)S(6)} %select_n.79), kind=kOutput, calls=%fused_computation.67 | convolution fusion | flops 15925248 | bytes 8020484 | tf_op jit(solution)/shard_map/dot_general | solution.py:23
  9.1 3.5 %constant_dynamic-slice_fusion.4 = bf16[576,2304]{1,0:T(8,128)(2,1)} fusion(bf16[576,4608]{1,0:T(8,128)(2,1)} %w1_mine.3, s32[]{:T(128)S(6)} %select_n.81), kind=kLoop, calls=%fused_computation.62 | loop fusion | bytes 5308420 | tf_op jit(solution)/shard_map/dynamic_slice | solution.py:43
  14.4 1.8 slice_bitcast_fusion.1
  19.3 1.9 collective-permute-done.2.gm_other_ref
  21.2 1.1 copy-done.16
  22.3 1.2 copy-done.19
  24.9 11.6 %front.1 = (bf16[2,256,1152]{2,1,0:T(8,128)(2,1)S(1)}, bf16[256,1152]{1,0:T(8,128)(2,1)S(1)}, bf16[256,1152]{1,0:T(8,128)(2,1)S(1)}, bf16[256,1152]{1,0:T(8,128)...) custom-call(s32[6]{0:T(128)S(1)} %stack.29.ids_ref, ...), custom_call_target="tpu_custom_call" | custom-call | flops 1000 | bytes 1000000 | tf_op jit(solution)/shard_map/front/pallas_call | solution.py:63
  38.5 1.6 collective-permute-done.5.h_other_ref
  40.6 1.2 copy-done.3
  41.8 16.5 %hidden.1 = (bf16[512,2304]{1,0:T(8,128)(2,1)S(1)}, bf16[512,2304]{1,0:T(8,128)(2,1)S(1)}, f32[1,2304]{1,0:T(1,128)S(1)}, bf16[8,72,2304]{2,1,0:T(8,128)(2,1)S(1)}, bf16[8,72,2304]{2,1,0:T(8,128)(2,1)S(1)}) custom-call(s32[6]{0:T(128)S(1)} %stack.29.ids_ref, bf16[256,1152]{1,0:T(8,128)(2,1)S(1)} %get-tuple-element.112.h_own_ref, ...), custom_call_target="tpu_custom_call" | custom-call | flops 1000 | bytes 1000000 | tf_op jit(solution)/shard_map/hidden/pallas_call | solution.py:63
  58.3 1.5 copy-done.60
  59.9 2.9 %collective-permute-start.11 = (bf16[8,72,2304]{2,1,0:T(8,128)(2,1)}, bf16[8,72,2304]{2,1,0:T(8,128)(2,1)S(1)}, u32[]{:S(2)}, u32[]{:S(2)}) collective-permute-start(bf16[8,72,2304]{2,1,0:T(8,128)(2,1)} %copy-done.60), channel_id=1, source_target_pairs={{0,2},{2,0},{4,6},{6,4},{8,10},{10,8},{12,14},{14,12},{16,18},{18,... | collective-permute-start | bytes 7962632 | tf_op jit(solution)/shard_map/ppermute | solution.py:644
  63.8 1.7 copy-done.1
  65.6 9.5 %partial.1 = (f32[2,256,1152]{2,1,0:T(8,128)S(1)}, f32[2,256,1152]{2,1,0:T(8,128)S(1)}) custom-call(s32[6]{0:T(128)S(1)} %stack.29.ids_ref, bf16[512,2304]{1,0:T(8,128)(2,1)S(1)} %get-tuple-element.116.act_ref.rest_0_, bf16[512,2304]{1,0:T(8,128)(2,1)S(1)} %get-tuple-element.117.gp_ref, bf16[576,4608]{1,0:T(8,128)(2,1)S(1)} %bitcast.62, ...), custom_call_target="tpu_custom_call" | custom-call | flops 1000 | bytes 1000000 | tf_op jit(solution)/shard_map/partial/pallas_call | solution.py:63
  75.3 10.3 %fc2_grad.1 = (bf16[4,2,48,1152]{3,2,1,0:T(8,128)(2,1)S(1)}, bf16[4,2,48,1152]{3,2,1,0:T(8,128)(2,1)}, bf16[4,2,96,1152]{3,2,1,0:T(8,128)(2,1)S(1)}, bf16[4,2,96,1152]{3,2,1,0:T(8,128)(2,1)}) custom-call(s32[6]{0:T(128)S(1)} %stack.29.ids_ref, bf16[256,1152]{1,0:T(8,128)(2,1)S(1)} %copy-done.4, bf16[256,1152]{1,0:T(8,128)(2,1)} %collective-permute-done.2.gm_other_ref, ...), custom_call_target="tpu_custom_call" | custom-call | flops 1000 | bytes 1000000 | tf_op jit(solution)/shard_map/fc2_grad/pallas_call | solution.py:63
  85.6 1.2 copy-done.10
  86.8 1.6 collective-permute-start.14
  88.4 13.2 %middle_back.1 = (f32[256,1152]{1,0:T(8,128)S(1)}, bf16[256,1152]{1,0:T(8,128)(2,1)S(1)}, bf16[256,1152]{1,0:T(8,128)(2,1)S(1)}, bf16[256,1152]{1,0:T(8,128)(2,1...) custom-call(s32[6]{0:T(128)S(1)} %stack.29.ids_ref, ...), custom_call_target="tpu_custom_call" | custom-call | flops 1000 | bytes 1000000 | tf_op jit(solution)/shard_map/middle_back/pallas_call | solution.py:63
  101.7 3.0 %advance.15 = (bf16[4,72,2304]{2,1,0:T(8,128)(2,1)}, bf16[4,72,2304]{2,1,0:T(8,128)(2,1)S(1)}) custom-call(s32[6]{0:T(128)S(1)} %stack.29.ids_ref, bf16[8,72,2304]{2,1,0:T(8,128)(2,1)S(1)} %get-tuple-element.130.keep_there.keep_here, bf16[8,72,2304]{2,1,0:T(8,128)(2,1)S(1)} %collective-permute-done.11.got_there.got_here, ...), custom_call_target="tpu_custom_call" | custom-call | flops 1000 | bytes 1000000 | tf_op jit(solution)/shard_map/advance/pallas_call | solution.py:372
  104.8 1.1 copy-done.12
  105.9 1.5 collective-permute-start.13
  108.9 1.6 collective-permute-done.12.g_got_ref
  110.4 1.1 copy-done.38
  111.5 1.3 copy-done.33
  112.8 1.3 copy-done.35
  114.1 1.3 copy-done.37
  115.3 1.3 copy-done.39
  116.6 7.1 %qkv_grad.1 = (bf16[8,72,1536]{2,1,0:T(8,128)(2,1)S(1)}, bf16[8,72,1536]{2,1,0:T(8,128)(2,1)}, bf16[8,72,768]{2,1,0:T(8,128)(2,1)S(1)}, bf16[8,72,768]{2,1,0:T(8,128)(2,1)}) custom-call(s32[6]{0:T(128)S(1)} %stack.29.ids_ref, bf16[256,2304]{1,0:T(8,128)(2,1)S(1)} %copy-done.37, bf16[256,2304]{1,0:T(8,128)(2,1)S(1)} %copy-done.39, ...), custom_call_target="tpu_custom_call" | custom-call | flops 1000 | bytes 1000000 | tf_op jit(solution)/shard_map/qkv_grad/pallas_call | solution.py:63
  124.4 5.9 %collective-permute-done.10.got_there.got_here = bf16[8,48,1152]{2,1,0:T(8,128)(2,1)} collective-permute-done((bf16[8,48,1152]{2,1,0:T(8,128)(2,1)}, bf16[8,48,1152]{2,1,0:T(8,128)(2,1)}, u32[]{:S(2)}, u32[]{:S(2)}) %collective-permute-start.10) | collective-permute-done | bytes 884768 | tf_op jit(solution)/shard_map/ppermute | solution.py:644
  130.3 4.1 %advance.16 = (bf16[4,48,1152]{2,1,0:T(8,128)(2,1)}, bf16[4,48,1152]{2,1,0:T(8,128)(2,1)S(1)}) custom-call(s32[6]{0:T(128)S(1)} %stack.29.ids_ref, bf16[8,48,1152]{2,1,0:T(8,128)(2,1)S(1)} %bitcast.67, bf16[8,48,1152]{2,1,0:T(8,128)(2,1)} %collective-permute-done.10.got_there.got_here, bf16[8,48,1152]{2,1,0:T(8,128)(2,1)S(1)} %bitcast.68, ...), custom_call_target="tpu_custom_call" | custom-call | flops 1000 | bytes 1000000 | tf_op jit(solution)/shard_map/advance/pallas_call | solution.py:372
  135.7 1.1 copy-done.45
  136.8 1.1 copy-done.47
  137.9 7.5 %last.1 = (bf16[256,1152]{1,0:T(8,128)(2,1)S(1)}, f32[256,1152]{1,0:T(8,128)S(1)}, f32[1,6912]{1,0:T(1,128)S(1)}) custom-call(s32[6]{0:T(128)S(1)} %stack.29.ids_ref, bf16[128,1152]{1,0:T(8,128)(2,1)S(1)} %copy-done.18, bf16[128,1152]{1,0:T(8,128)(2,1)S(1)} %copy-done.21, bf16[128,1152]{1,0:T(8,128)(2,1)S(1)} %get-tuple-element.213.cot_mine_ref, ...), custom_call_target="tpu_custom_call" | custom-call | flops 1000 | bytes 1000000 | tf_op jit(solution)/shard_map/last/pallas_call | solution.py:63
  145.9 4.2 %advance.17 = (bf16[4,96,1152]{2,1,0:T(8,128)(2,1)}, bf16[4,96,1152]{2,1,0:T(8,128)(2,1)S(1)}) custom-call(s32[6]{0:T(128)S(1)} %stack.29.ids_ref, bf16[8,96,1152]{2,1,0:T(8,128)(2,1)S(1)} %bitcast.65, bf16[8,96,1152]{2,1,0:T(8,128)(2,1)} %collective-permute-done.14.got_there.got_here, bf16[8,96,1152]{2,1,0:T(8,128)(2,1)S(1)} %bitcast.66, ...), custom_call_target="tpu_custom_call" | custom-call | flops 1000 | bytes 1000000 | tf_op jit(solution)/shard_map/advance/pallas_call | solution.py:372
  150.2 1.1 collective-permute-start.20
  151.2 2.0 advance.18
  154.9 1.8 all-gather
  157.3 2.7 %collective-permute-start.15 = (bf16[2,8064]{1,0:T(2,128)(2,1)S(1)}, bf16[2,8064]{1,0:T(2,128)(2,1)S(1)}, u32[]{:S(2)}, u32[]{:S(2)}) collective-permute-start(bf16[2,8064]{1,0:T(2,128)(2,1)S(1)} %pad_maximum_fusion.8), channel_id=1, source_target_pairs={{0,16},{2,18},{4,20},{6,22},{8,24},{10,26},{12,28},{14,30},{16,0},... | collective-permute-start | bytes 96776 | tf_op jit(solution)/shard_map/ppermute | solution.py:665
  160.1 5.4 %convolution_bitcast_fusion = f32[1,576,2]{1,2,0:T(2,128)S(1)} fusion(bf16[576,6912]{1,0:T(8,128)(2,1)} %param.17, bf16[2,1,6912]{2,1,0:T(2,128)(2,1)S(1)} %all-gather), kind=kOutput, calls=%fused_computation.2 | convolution fusion | flops 15925248 | bytes 7994880 | tf_op jit(solution)/shard_map/dot_general | solution.py:31
  165.4 2.0 all-gather.1
  168.2 1.6 collective-permute-start.26
  169.8 3.2 %advance.19 = (bf16[4,72,1536]{2,1,0:T(8,128)(2,1)S(1)}, bf16[4,72,1536]{2,1,0:T(8,128)(2,1)S(1)}) custom-call(s32[6]{0:T(128)S(1)} %stack.29.ids_ref, bf16[8,72,1536]{2,1,0:T(8,128)(2,1)S(1)} %get-tuple-element.158.keep_there.keep_here, bf16[8,72,1536]{2,1,0:T(8,128)(2,1)} %collective-permute-done.17.got_there.got_here, ...), custom_call_target="tpu_custom_call" | custom-call | flops 1000 | bytes 1000000 | tf_op jit(solution)/shard_map/advance/pallas_call | solution.py:372
  173.0 1.1 collective-permute-start.25
  174.1 2.8 %advance.20 = (bf16[4,72,768]{2,1,0:T(8,128)(2,1)S(1)}, bf16[4,72,768]{2,1,0:T(8,128)(2,1)S(1)}) custom-call(s32[6]{0:T(128)S(1)} %stack.29.ids_ref, bf16[8,72,768]{2,1,0:T(8,128)(2,1)S(1)} %copy-done.25, bf16[8,72,768]{2,1,0:T(8,128)(2,1)} %collective-permute-done.16.got_there.got_here, bf16[8,72,768]{2,1,0:T(8,128)(2,1)S(1)} %copy-done.25, ...), custom_call_target="tpu_custom_call" | custom-call | flops 1000 | bytes 1000000 | tf_op jit(solution)/shard_map/advance/pallas_call | solution.py:372
  177.5 1.5 collective-permute-start.24
  179.0 1.7 advance.21
  180.7 1.7 collective-permute-start.29
  182.4 2.0 advance.22
  184.4 3.1 %collective-permute-done.19 = bf16[4,8064]{1,0:T(4,128)(2,1)S(1)} collective-permute-done((bf16[4,8064]{1,0:T(4,128)(2,1)S(1)}, bf16[4,8064]{1,0:T(4,128)(2,1)S(1)}, u32[]{:S(2)}, u32[]{:S(2)}) %collective-permute-start.19) | collective-permute-done | bytes 64544 | tf_op jit(solution)/shard_map/ppermute | solution.py:665
  195.4 3.2 %collective-permute-done.23 = bf16[8,8064]{1,0:T(8,128)(2,1)S(1)} collective-permute-done((bf16[8,8064]{1,0:T(8,128)(2,1)S(1)}, bf16[8,8064]{1,0:T(8,128)(2,1)S(1)}, u32[]{:S(2)}, u32[]{:S(2)}) %collective-permute-start.23) | collective-permute-done | bytes 129056 | tf_op jit(solution)/shard_map/ppermute | solution.py:665
  199.9 1.1 pad_maximum_fusion
  201.0 1.6 collective-permute-start.30
  202.6 1.5 collective-permute-start.35
  204.1 1.2 advance.26
  206.4 1.7 collective-permute-done.27
  209.7 3.8 %concatenate.59 = bf16[32,8064]{1,0:T(8,128)(2,1)} concatenate(bf16[2,8064]{1,0:T(2,128)(2,1)} %copy-done.76, bf16[2,8064]{1,0:T(2,128)(2,1)S(1)} %copy-done.69, bf16[4,8064]{1,0:T(4,128)(2,1)S(1)} %copy-done.64, bf16[8,8064]{1,0:T(8,128)(2,1)S(1)} %copy-done.66, bf16[16,8064]{1,0:T(8,128)(2,1)} %copy-done.72), dimensions={0} | concatenate | bytes 1032192 | tf_op jit(solution)/shard_map/concatenate | solution.py:668
  216.0 2.0 reshape.90
  220.4 2.4 psum.7
  222.8 1.9 add_bitcast_fusion
  224.7 2.3 fusion.2
  230.1 2.1 collective-permute-start.32
  236.7 9.5 %collective-permute-done.32 = bf16[1,72,1536]{2,1,0:T(8,128)(2,1)S(1)} collective-permute-done((bf16[1,72,1536]{2,1,0:T(8,128)(2,1)S(1)}, bf16[1,72,1536]{2,1,0:T(8,128)(2,1)S(1)}, u32[]{:S(2)}, u32[]{:S(2)}) %collective-permute-start.32) | collective-permute-done | bytes 221216 | tf_op jit(solution)/shard_map/ppermute | solution.py:644
  246.3 1.8 collective-permute-done.36
  (296 shorter events, 45.2 us)
Async XLA Ops:
  3.6 10.8 %collective-permute-start = (bf16[2,128,1152]{2,1,0:T(8,128)(2,1)}, bf16[2,128,1152]{2,1,0:T(8,128)(2,1)}, u32[]{:S(2)}, u32[]{:S(2)}) collective-permute-start(bf16[2,128,1152]{2,1,0:T(8,128)(2,1)} %pad_maximum_fusion.2), channel_id=1, source_target_pairs={{0,1},{1,0},{2,3},{3,2},{4,5},{5,4},{6,7},{7,6},{8,9},{9,8},{10,11... | collective-permute-start | bytes 1769480 | tf_op jit(solution)/shard_map/ppermute | solution.py:35
  8.5 5.8 %collective-permute-start.1 = (f32[2,6912]{1,0:T(2,128)S(1)}, f32[2,6912]{1,0:T(2,128)S(1)}, u32[]{:S(2)}, u32[]{:S(2)}) collective-permute-start(f32[2,6912]{1,0:T(2,128)S(1)} %fusion.15), channel_id=1, source_target_pairs={{0,1},{1,0},{2,3},{3,2},{4,5},{5,4},{6,7},{7,6},{8,9},{9,8},{10,11... | collective-permute-start | bytes 165896 | tf_op jit(solution)/shard_map/ppermute | solution.py:35
  8.6 12.6 %collective-permute-start.3 = (bf16[576,3456]{1,0:T(8,128)(2,1)}, bf16[576,3456]{1,0:T(8,128)(2,1)}, u32[]{:S(2)}, u32[]{:S(2)}) collective-permute-start(bf16[576,3456]{1,0:T(8,128)(2,1)} %wq_mine.3), channel_id=1, source_target_pairs={{0,1},{1,0},{2,3},{3,2},{4,5},{5,4},{6,7},{7,6},{8,9},{9,8},{10,11... | collective-permute-start | bytes 11943944 | tf_op jit(solution)/shard_map/ppermute | solution.py:35
  9.0 12.1 %collective-permute-start.4 = (bf16[576,1152]{1,0:T(8,128)(2,1)}, bf16[576,1152]{1,0:T(8,128)(2,1)}, u32[]{:S(2)}, u32[]{:S(2)}) collective-permute-start(bf16[576,1152]{1,0:T(8,128)(2,1)} %wp_mine.3), channel_id=1, source_target_pairs={{0,1},{1,0},{2,3},{3,2},{4,5},{5,4},{6,7},{7,6},{8,9},{9,8},{10,11... | collective-permute-start | bytes 3981320 | tf_op jit(solution)/shard_map/ppermute | solution.py:35
  12.6 28.0 %collective-permute-start.6 = (bf16[576,2304]{1,0:T(8,128)(2,1)}, bf16[576,2304]{1,0:T(8,128)(2,1)S(1)}, u32[]{:S(2)}, u32[]{:S(2)}) collective-permute-start(bf16[576,2304]{1,0:T(8,128)(2,1)} %constant_dynamic-slice_fusion.4), channel_id=1, source_target_pairs={{0,1},{1,0},{2,3},{3,2},{4,5},{5,4},{6,7},{7,6},{8,9},{9,8},{10,11... | collective-permute-start | bytes 7962632 | tf_op jit(solution)/shard_map/ppermute | solution.py:35
  17.2 19.3 %copy-start.2 = (bf16[256,1152]{1,0:T(8,128)(2,1)}, bf16[256,1152]{1,0:T(8,128)(2,1)S(1)}, u32[]{:S(2)}) copy-start(bf16[256,1152]{1,0:T(8,128)(2,1)S(1)} %multiply_convert_fusion.gm_own_ref) | copy-start | bytes 1769476
  17.2 4.0 %collective-permute-start.2 = (bf16[256,1152]{1,0:T(8,128)(2,1)S(1)}, bf16[256,1152]{1,0:T(8,128)(2,1)}, u32[]{:S(2)}, u32[]{:S(2)}) collective-permute-start(bf16[256,1152]{1,0:T(8,128)(2,1)S(1)} %multiply_convert_fusion.gm_own_ref), channel_id=1, source_target_pairs={{0,1},{1,0},{2,3},{3,2},{4,5},{5,4},{6,7},{7,6},{8,9},{9,8},{10,11... | collective-permute-start | bytes 1769480 | tf_op jit(solution)/shard_map/ppermute | solution.py:35
  21.1 19.4 %slice-start = ((s8[5308416]{0:T(1024)(128)(4,1)}), s8[4194304]{0:T(1024)(128)(4,1)S(1)}, s32[]{:S(2)}) async-start(s8[5308416]{0:T(1024)(128)(4,1)} %bitcast.61), calls=%async_computation | async-start | bytes 8388608
  24.9 15.6 %copy-start.82 = (bf16[4608]{0:T(1024)(128)(2,1)S(1)}, bf16[4608]{0:T(1024)(128)(2,1)}, u32[]{:S(2)}) copy-start(bf16[4608]{0:T(1024)(128)(2,1)} %param.24) | copy-start | bytes 27652
  24.9 15.7 %slice-start.1 = ((s8[5308416]{0:T(1024)(128)(4,1)}), s8[1114112]{0:T(1024)(128)(4,1)S(1)}, s32[]{:S(2)}) async-start(s8[5308416]{0:T(1024)(128)(4,1)} %bitcast.61), calls=%async_computation.1 | async-start | bytes 2228224
  38.1 20.1 %copy-start.32 = (bf16[2,256,1152]{2,1,0:T(8,128)(2,1)}, bf16[2,256,1152]{2,1,0:T(8,128)(2,1)S(1)}, u32[]{:S(2)}) copy-start(bf16[2,256,1152]{2,1,0:T(8,128)(2,1)S(1)} %get-tuple-element.115.both_ref) | copy-start | bytes 3538948
  38.1 20.1 %copy-start.48 = (bf16[256,1152]{1,0:T(8,128)(2,1)}, bf16[256,1152]{1,0:T(8,128)(2,1)S(1)}, u32[]{:S(2)}) copy-start(bf16[256,1152]{1,0:T(8,128)(2,1)S(1)} %get-tuple-element.123.q_ref) | copy-start | bytes 1769476
  38.1 50.3 %copy-start.14 = (f32[256,1152]{1,0:T(8,128)}, f32[256,1152]{1,0:T(8,128)S(1)}, u32[]{:S(2)}) copy-start(f32[256,1152]{1,0:T(8,128)S(1)} %get-tuple-element.111.attn_ref) | copy-start | bytes 3538948
  38.1 2.0 collective-permute-start.5
  40.1 22.7 %collective-permute-start.7 = (bf16[2,256,1152]{2,1,0:T(8,128)(2,1)S(1)}, bf16[2,256,1152]{2,1,0:T(8,128)(2,1)S(1)}, u32[]{:S(2)}, u32[]{:S(2)}) collective-permute-start(bf16[2,256,1152]{2,1,0:T(8,128)(2,1)S(1)} %get-tuple-element.115.both_ref), channel_id=1, source_target_pairs={{0,1},{1,0},{2,3},{3,2},{4,5},{5,4},{6,7},{7,6},{8,9},{9,8},{10,11... | collective-permute-start | bytes 3538952 | tf_op jit(solution)/shard_map/ppermute | solution.py:35
  40.5 23.3 %slice-start.2 = ((s8[5308416]{0:T(1024)(128)(4,1)}), s8[4194304]{0:T(1024)(128)(4,1)S(1)}, s32[]{:S(2)}) async-start(s8[5308416]{0:T(1024)(128)(4,1)} %bitcast.63), calls=%async_computation.2 | async-start | bytes 8388608
  40.5 23.3 %slice-start.3 = ((s8[5308416]{0:T(1024)(128)(4,1)}), s8[1114112]{0:T(1024)(128)(4,1)S(1)}, s32[]{:S(2)}) async-start(s8[5308416]{0:T(1024)(128)(4,1)} %bitcast.63), calls=%async_computation.3 | async-start | bytes 2228224
  41.8 16.5 %copy-start = (bf16[576,2304]{1,0:T(8,128)(2,1)}, bf16[576,2304]{1,0:T(8,128)(2,1)S(1)}, u32[]{:S(2)}) copy-start(bf16[576,2304]{1,0:T(8,128)(2,1)S(1)} %collective-permute-done.6.w1_theirs) | copy-start | bytes 7962628
  59.8 15.5 %collective-permute-start.9 = (bf16[512,2304]{1,0:T(8,128)(2,1)S(1)}, bf16[512,2304]{1,0:T(8,128)(2,1)}, u32[]{:S(2)}, u32[]{:S(2)}) collective-permute-start(bf16[512,2304]{1,0:T(8,128)(2,1)S(1)} %get-tuple-element.116.act_ref.rest_0_), channel_id=1, source_target_pairs={{0,1},{1,0},{2,3},{3,2},{4,5},{5,4},{6,7},{7,6},{8,9},{9,8},{10,11... | collective-permute-start | bytes 7077896 | tf_op jit(solution)/shard_map/ppermute | solution.py:35
  59.9 41.8 %collective-permute-start.11 = (bf16[8,72,2304]{2,1,0:T(8,128)(2,1)}, bf16[8,72,2304]{2,1,0:T(8,128)(2,1)S(1)}, u32[]{:S(2)}, u32[]{:S(2)}) collective-permute-start(bf16[8,72,2304]{2,1,0:T(8,128)(2,1)} %copy-done.60), channel_id=1, source_target_pairs={{0,2},{2,0},{4,6},{6,4},{8,10},{10,8},{12,14},{14,12},{16,18},{18,... | collective-permute-start | bytes 7962632 | tf_op jit(solution)/shard_map/ppermute | solution.py:644
  75.1 13.3 %copy-start.6 = (f32[2,256,1152]{2,1,0:T(8,128)}, f32[2,256,1152]{2,1,0:T(8,128)S(1)}, u32[]{:S(2)}) copy-start(f32[2,256,1152]{2,1,0:T(8,128)S(1)} %get-tuple-element.122.part_ref) | copy-start | bytes 7077892
  75.1 13.3 %copy-start.17 = (bf16[128,1152]{1,0:T(8,128)(2,1)S(1)}, bf16[128,1152]{1,0:T(8,128)(2,1)}, u32[]{:S(2)}) copy-start(bf16[128,1152]{1,0:T(8,128)(2,1)} %get-tuple-element.110.mine_ref) | copy-start | bytes 884740
  75.1 13.3 %copy-start.20 = (bf16[128,1152]{1,0:T(8,128)(2,1)S(1)}, bf16[128,1152]{1,0:T(8,128)(2,1)}, u32[]{:S(2)}) copy-start(bf16[128,1152]{1,0:T(8,128)(2,1)} %get-tuple-element.212.theirs_ref) | copy-start | bytes 884740
  75.1 13.3 %copy-start.23 = (bf16[128,1152]{1,0:T(8,128)(2,1)S(1)}, bf16[128,1152]{1,0:T(8,128)(2,1)}, u32[]{:S(2)}) copy-start(bf16[128,1152]{1,0:T(8,128)(2,1)} %copy-done.22) | copy-start | bytes 884740
  75.1 13.3 %copy-start.49 = (bf16[256,1152]{1,0:T(8,128)(2,1)S(1)}, bf16[256,1152]{1,0:T(8,128)(2,1)}, u32[]{:S(2)}) copy-start(bf16[256,1152]{1,0:T(8,128)(2,1)} %copy-done.48) | copy-start | bytes 1769476
  75.1 13.3 %copy-start.51 = (bf16[256,1152]{1,0:T(8,128)(2,1)S(1)}, bf16[256,1152]{1,0:T(8,128)(2,1)}, u32[]{:S(2)}) copy-start(bf16[256,1152]{1,0:T(8,128)(2,1)} %copy-done.50) | copy-start | bytes 1769476
  75.1 13.3 %copy-start.53 = (bf16[256,1152]{1,0:T(8,128)(2,1)S(1)}, bf16[256,1152]{1,0:T(8,128)(2,1)}, u32[]{:S(2)}) copy-start(bf16[256,1152]{1,0:T(8,128)(2,1)} %copy-done.52) | copy-start | bytes 1769476
  75.2 13.3 %copy-start.58 = (f32[1,6912]{1,0:T(1,128)S(1)}, f32[1,6912]{1,0:T(1,128)}, u32[]{:S(2)}) copy-start(f32[1,6912]{1,0:T(1,128)} %copy-done.56) | copy-start | bytes 82948
  75.2 13.2 %collective-permute-start.8 = (f32[2,256,1152]{2,1,0:T(8,128)S(1)}, f32[2,256,1152]{2,1,0:T(8,128)S(1)}, u32[]{:S(2)}, u32[]{:S(2)}) collective-permute-start(f32[2,256,1152]{2,1,0:T(8,128)S(1)} %get-tuple-element.119), channel_id=1, source_target_pairs={{0,1},{1,0},{2,3},{3,2},{4,5},{5,4},{6,7},{7,6},{8,9},{9,8},{10,11... | collective-permute-start | bytes 7077896 | tf_op jit(solution)/shard_map/ppermute | solution.py:35
  86.8 58.6 %collective-permute-start.14 = (bf16[8,96,1152]{2,1,0:T(8,128)(2,1)}, bf16[8,96,1152]{2,1,0:T(8,128)(2,1)}, u32[]{:S(2)}, u32[]{:S(2)}) collective-permute-start(bf16[8,96,1152]{2,1,0:T(8,128)(2,1)} %bitcast.14), channel_id=1, source_target_pairs={{0,8},{2,10},{4,12},{6,14},{8,0},{10,2},{12,4},{14,6},{16,24},{18,... | collective-permute-start | bytes 5308424 | tf_op jit(solution)/shard_map/ppermute | solution.py:644
  88.4 13.3 %copy-start.8 = (f32[2,256,1152]{2,1,0:T(8,128)}, f32[2,256,1152]{2,1,0:T(8,128)S(1)}, u32[]{:S(2)}) copy-start(f32[2,256,1152]{2,1,0:T(8,128)S(1)} %collective-permute-done.8.got_ref) | copy-start | bytes 7077892
  105.9 45.4 %collective-permute-start.13 = (bf16[4,72,2304]{2,1,0:T(8,128)(2,1)}, bf16[4,72,2304]{2,1,0:T(8,128)(2,1)}, u32[]{:S(2)}, u32[]{:S(2)}) collective-permute-start(bf16[4,72,2304]{2,1,0:T(8,128)(2,1)} %get-tuple-element.134), channel_id=1, source_target_pairs={{0,4},{2,6},{4,0},{6,2},{8,12},{10,14},{12,8},{14,10},{16,20},{18,... | collective-permute-start | bytes 3981320 | tf_op jit(solution)/shard_map/ppermute | solution.py:644
  107.4 3.1 %collective-permute-start.12 = (bf16[256,2304]{1,0:T(8,128)(2,1)}, bf16[256,2304]{1,0:T(8,128)(2,1)S(1)}, u32[]{:S(2)}, u32[]{:S(2)}) collective-permute-start(bf16[256,2304]{1,0:T(8,128)(2,1)} %get-tuple-element.132), channel_id=1, source_target_pairs={{0,1},{1,0},{2,3},{3,2},{4,5},{5,4},{6,7},{7,6},{8,9},{9,8},{10,11... | collective-permute-start | bytes 3538952 | tf_op jit(solution)/shard_map/ppermute | solution.py:35
  107.4 22.9 %collective-permute-start.10 = (bf16[8,48,1152]{2,1,0:T(8,128)(2,1)}, bf16[8,48,1152]{2,1,0:T(8,128)(2,1)}, u32[]{:S(2)}, u32[]{:S(2)}) collective-permute-start(bf16[8,48,1152]{2,1,0:T(8,128)(2,1)} %bitcast.11), channel_id=1, source_target_pairs={{0,2},{2,0},{4,6},{6,4},{8,10},{10,8},{12,14},{14,12},{16,18},{18,... | collective-permute-start | bytes 2654216 | tf_op jit(solution)/shard_map/ppermute | solution.py:644
  116.6 19.1 %copy-start.9 = (f32[2,256,1152]{2,1,0:T(8,128)S(1)}, f32[2,256,1152]{2,1,0:T(8,128)}, u32[]{:S(2)}) copy-start(f32[2,256,1152]{2,1,0:T(8,128)} %copy-done.8) | copy-start | bytes 7077892
  116.6 19.1 %copy-start.18 = (bf16[128,1152]{1,0:T(8,128)(2,1)S(1)}, bf16[128,1152]{1,0:T(8,128)(2,1)}, u32[]{:S(2)}) copy-start(bf16[128,1152]{1,0:T(8,128)(2,1)} %get-tuple-element.110.mine_ref) | copy-start | bytes 884740
  116.6 19.1 %copy-start.21 = (bf16[128,1152]{1,0:T(8,128)(2,1)S(1)}, bf16[128,1152]{1,0:T(8,128)(2,1)}, u32[]{:S(2)}) copy-start(bf16[128,1152]{1,0:T(8,128)(2,1)} %get-tuple-element.212.theirs_ref) | copy-start | bytes 884740
  116.6 19.1 %copy-start.31 = (f32[256,1152]{1,0:T(8,128)S(1)}, f32[256,1152]{1,0:T(8,128)}, u32[]{:S(2)}) copy-start(f32[256,1152]{1,0:T(8,128)} %copy-done.30) | copy-start | bytes 3538948
  116.6 19.1 %copy-start.43 = (bf16[256,1152]{1,0:T(8,128)(2,1)S(1)}, bf16[256,1152]{1,0:T(8,128)(2,1)}, u32[]{:S(2)}) copy-start(bf16[256,1152]{1,0:T(8,128)(2,1)} %copy-done.42) | copy-start | bytes 1769476
  123.8 44.5 %collective-permute-start.17 = (bf16[8,72,1536]{2,1,0:T(8,128)(2,1)}, bf16[8,72,1536]{2,1,0:T(8,128)(2,1)}, u32[]{:S(2)}, u32[]{:S(2)}) collective-permute-start(bf16[8,72,1536]{2,1,0:T(8,128)(2,1)} %get-tuple-element.136), channel_id=1, source_target_pairs={{0,2},{2,0},{4,6},{6,4},{8,10},{10,8},{12,14},{14,12},{16,18},{18,... | collective-permute-start | bytes 5308424 | tf_op jit(solution)/shard_map/ppermute | solution.py:644
  135.2 42.3 %collective-permute-start.21 = (bf16[4,48,1152]{2,1,0:T(8,128)(2,1)}, bf16[4,48,1152]{2,1,0:T(8,128)(2,1)}, u32[]{:S(2)}, u32[]{:S(2)}) collective-permute-start(bf16[4,48,1152]{2,1,0:T(8,128)(2,1)} %get-tuple-element.138), channel_id=1, source_target_pairs={{0,4},{2,6},{4,0},{6,2},{8,12},{10,14},{12,8},{14,10},{16,20},{18,... | collective-permute-start | bytes 1327112 | tf_op jit(solution)/shard_map/ppermute | solution.py:644
  145.4 27.6 %collective-permute-start.16 = (bf16[8,72,768]{2,1,0:T(8,128)(2,1)}, bf16[8,72,768]{2,1,0:T(8,128)(2,1)}, u32[]{:S(2)}, u32[]{:S(2)}) collective-permute-start(bf16[8,72,768]{2,1,0:T(8,128)(2,1)} %get-tuple-element.157), channel_id=1, source_target_pairs={{0,8},{2,10},{4,12},{6,14},{8,0},{10,2},{12,4},{14,6},{16,24},{18,... | collective-permute-start | bytes 2654216 | tf_op jit(solution)/shard_map/ppermute | solution.py:644
  150.2 30.6 %collective-permute-start.20 = (bf16[4,96,1152]{2,1,0:T(8,128)(2,1)}, bf16[4,96,1152]{2,1,0:T(8,128)(2,1)}, u32[]{:S(2)}, u32[]{:S(2)}) collective-permute-start(bf16[4,96,1152]{2,1,0:T(8,128)(2,1)} %get-tuple-element.150), channel_id=1, source_target_pairs={{0,2},{2,0},{4,6},{6,4},{8,10},{10,8},{12,14},{14,12},{16,18},{18,... | collective-permute-start | bytes 2654216 | tf_op jit(solution)/shard_map/ppermute | solution.py:644
  156.8 31.7 %copy-start.70 = (bf16[2,1,3456]{2,0,1:T(2,128)(2,1)}, bf16[2,1,3456]{2,0,1:T(2,128)(2,1)S(1)}, u32[]{:S(2)}) copy-start(bf16[2,1,3456]{2,0,1:T(2,128)(2,1)S(1)} %copy.36) | copy-start | bytes 41476
  157.3 19.5 %collective-permute-start.15 = (bf16[2,8064]{1,0:T(2,128)(2,1)S(1)}, bf16[2,8064]{1,0:T(2,128)(2,1)S(1)}, u32[]{:S(2)}, u32[]{:S(2)}) collective-permute-start(bf16[2,8064]{1,0:T(2,128)(2,1)S(1)} %pad_maximum_fusion.8), channel_id=1, source_target_pairs={{0,16},{2,18},{4,20},{6,22},{8,24},{10,26},{12,28},{14,30},{16,0},... | collective-permute-start | bytes 96776 | tf_op jit(solution)/shard_map/ppermute | solution.py:665
  168.2 20.5 %collective-permute-start.26 = (bf16[2,72,2304]{2,1,0:T(8,128)(2,1)}, bf16[2,72,2304]{2,1,0:T(8,128)(2,1)S(1)}, u32[]{:S(2)}, u32[]{:S(2)}) collective-permute-start(bf16[2,72,2304]{2,1,0:T(8,128)(2,1)} %copy-done.61), channel_id=1, source_target_pairs={{0,8},{2,10},{4,12},{6,14},{8,0},{10,2},{12,4},{14,6},{16,24},{18,... | collective-permute-start | bytes 1990664 | tf_op jit(solution)/shard_map/ppermute | solution.py:644
  173.0 20.5 %collective-permute-start.25 = (bf16[4,72,1536]{2,1,0:T(8,128)(2,1)S(1)}, bf16[4,72,1536]{2,1,0:T(8,128)(2,1)S(1)}, u32[]{:S(2)}, u32[]{:S(2)}) collective-permute-start(bf16[4,72,1536]{2,1,0:T(8,128)(2,1)S(1)} %get-tuple-element.160), channel_id=1, source_target_pairs={{0,4},{2,6},{4,0},{6,2},{8,12},{10,14},{12,8},{14,10},{16,20},{18,... | collective-permute-start | bytes 2654216 | tf_op jit(solution)/shard_map/ppermute | solution.py:644
  176.9 11.7 %copy-start.67 = (bf16[2,8064]{1,0:T(2,128)(2,1)}, bf16[2,8064]{1,0:T(2,128)(2,1)S(1)}, u32[]{:S(2)}) copy-start(bf16[2,8064]{1,0:T(2,128)(2,1)S(1)} %collective-permute-done.15) | copy-start | bytes 96772
  177.0 10.6 %collective-permute-start.19 = (bf16[4,8064]{1,0:T(4,128)(2,1)S(1)}, bf16[4,8064]{1,0:T(4,128)(2,1)S(1)}, u32[]{:S(2)}, u32[]{:S(2)}) collective-permute-start(bf16[4,8064]{1,0:T(4,128)(2,1)S(1)} %pad_maximum_fusion.7), channel_id=1, source_target_pairs={{0,8},{2,10},{4,12},{6,14},{8,0},{10,2},{12,4},{14,6},{16,24},{18,... | collective-permute-start | bytes 193544 | tf_op jit(solution)/shard_map/ppermute | solution.py:665
  177.5 17.2 %collective-permute-start.24 = (bf16[4,72,768]{2,1,0:T(8,128)(2,1)S(1)}, bf16[4,72,768]{2,1,0:T(8,128)(2,1)S(1)}, u32[]{:S(2)}, u32[]{:S(2)}) collective-permute-start(bf16[4,72,768]{2,1,0:T(8,128)(2,1)S(1)} %get-tuple-element.162), channel_id=1, source_target_pairs={{0,2},{2,0},{4,6},{6,4},{8,10},{10,8},{12,14},{14,12},{16,18},{18,... | collective-permute-start | bytes 1327112 | tf_op jit(solution)/shard_map/ppermute | solution.py:644
  180.7 21.8 %collective-permute-start.29 = (bf16[2,48,1152]{2,1,0:T(8,128)(2,1)S(1)}, bf16[2,48,1152]{2,1,0:T(8,128)(2,1)S(1)}, u32[]{:S(2)}, u32[]{:S(2)}) collective-permute-start(bf16[2,48,1152]{2,1,0:T(8,128)(2,1)S(1)} %get-tuple-element.169), channel_id=1, source_target_pairs={{0,8},{2,10},{4,12},{6,14},{8,0},{10,2},{12,4},{14,6},{16,24},{18,... | collective-permute-start | bytes 663560 | tf_op jit(solution)/shard_map/ppermute | solution.py:644
  187.6 11.1 %copy-start.63 = (bf16[4,8064]{1,0:T(4,128)(2,1)}, bf16[4,8064]{1,0:T(4,128)(2,1)S(1)}, u32[]{:S(2)}) copy-start(bf16[4,8064]{1,0:T(4,128)(2,1)S(1)} %collective-permute-done.19) | copy-start | bytes 193540
  187.6 17.8 %collective-permute-start.28 = (bf16[2,96,1152]{2,1,0:T(8,128)(2,1)S(1)}, bf16[2,96,1152]{2,1,0:T(8,128)(2,1)S(1)}, u32[]{:S(2)}, u32[]{:S(2)}) collective-permute-start(bf16[2,96,1152]{2,1,0:T(8,128)(2,1)S(1)} %get-tuple-element.171), channel_id=1, source_target_pairs={{0,4},{2,6},{4,0},{6,2},{8,12},{10,14},{12,8},{14,10},{16,20},{18,... | collective-permute-start | bytes 1327112 | tf_op jit(solution)/shard_map/ppermute | solution.py:644
  188.7 1.6 collective-permute-start.18
  190.3 2.0 collective-permute-start.22
  192.3 6.3 %collective-permute-start.23 = (bf16[8,8064]{1,0:T(8,128)(2,1)S(1)}, bf16[8,8064]{1,0:T(8,128)(2,1)S(1)}, u32[]{:S(2)}, u32[]{:S(2)}) collective-permute-start(bf16[8,8064]{1,0:T(8,128)(2,1)S(1)} %pad_maximum_fusion.6), channel_id=1, source_target_pairs={{0,4},{2,6},{4,0},{6,2},{8,12},{10,14},{12,8},{14,10},{16,20},{18,... | collective-permute-start | bytes 387080 | tf_op jit(solution)/shard_map/ppermute | solution.py:665
  193.5 22.5 %collective-permute-start.31 = (bf16[1,72,2304]{2,1,0:T(8,128)(2,1)S(1)}, bf16[1,72,2304]{2,1,0:T(8,128)(2,1)}, u32[]{:S(2)}, u32[]{:S(2)}) collective-permute-start(bf16[1,72,2304]{2,1,0:T(8,128)(2,1)S(1)} %get-tuple-element.178), channel_id=1, source_target_pairs={{0,16},{2,18},{4,20},{6,22},{8,24},{10,26},{12,28},{14,30},{16,0},... | collective-permute-start | bytes 995336 | tf_op jit(solution)/shard_map/ppermute | solution.py:644
  198.8 9.2 %collective-permute-start.27 = (bf16[16,8064]{1,0:T(8,128)(2,1)S(1)}, bf16[16,8064]{1,0:T(8,128)(2,1)S(1)}, u32[]{:S(2)}, u32[]{:S(2)}) collective-permute-start(bf16[16,8064]{1,0:T(8,128)(2,1)S(1)} %pad_maximum_fusion.5), channel_id=1, source_target_pairs={{0,2},{2,0},{4,6},{6,4},{8,10},{10,8},{12,14},{14,12},{16,18},{18,... | collective-permute-start | bytes 774152 | tf_op jit(solution)/shard_map/ppermute | solution.py:665
  201.0 28.5 %collective-permute-start.30 = (bf16[2,72,1536]{2,1,0:T(8,128)(2,1)S(1)}, bf16[2,72,1536]{2,1,0:T(8,128)(2,1)S(1)}, u32[]{:S(2)}, u32[]{:S(2)}) collective-permute-start(bf16[2,72,1536]{2,1,0:T(8,128)(2,1)S(1)} %get-tuple-element.180), channel_id=1, source_target_pairs={{0,8},{2,10},{4,12},{6,14},{8,0},{10,2},{12,4},{14,6},{16,24},{18,... | collective-permute-start | bytes 1327112 | tf_op jit(solution)/shard_map/ppermute | solution.py:644
  202.6 29.6 %collective-permute-start.35 = (bf16[2,72,768]{2,1,0:T(8,128)(2,1)S(1)}, bf16[2,72,768]{2,1,0:T(8,128)(2,1)S(1)}, u32[]{:S(2)}, u32[]{:S(2)}) collective-permute-start(bf16[2,72,768]{2,1,0:T(8,128)(2,1)S(1)} %get-tuple-element.182), channel_id=1, source_target_pairs={{0,4},{2,6},{4,0},{6,2},{8,12},{10,14},{12,8},{14,10},{16,20},{18,... | collective-permute-start | bytes 663560 | tf_op jit(solution)/shard_map/ppermute | solution.py:644
  205.3 28.4 %collective-permute-start.34 = (bf16[1,48,1152]{2,1,0:T(8,128)(2,1)}, bf16[1,48,1152]{2,1,0:T(8,128)(2,1)}, u32[]{:S(2)}, u32[]{:S(2)}) collective-permute-start(bf16[1,48,1152]{2,1,0:T(8,128)(2,1)} %get-tuple-element.187), channel_id=1, source_target_pairs={{0,16},{2,18},{4,20},{6,22},{8,24},{10,26},{12,28},{14,30},{16,0},... | collective-permute-start | bytes 331784 | tf_op jit(solution)/shard_map/ppermute | solution.py:644
  208.8 25.9 %collective-permute-start.33 = (bf16[1,96,1152]{2,1,0:T(8,128)(2,1)S(1)}, bf16[1,96,1152]{2,1,0:T(8,128)(2,1)}, u32[]{:S(2)}, u32[]{:S(2)}) collective-permute-start(bf16[1,96,1152]{2,1,0:T(8,128)(2,1)S(1)} %get-tuple-element.189), channel_id=1, source_target_pairs={{0,16},{2,18},{4,20},{6,22},{8,24},{10,26},{12,28},{14,30},{16,0},... | collective-permute-start | bytes 663560 | tf_op jit(solution)/shard_map/ppermute | solution.py:644
  230.1 16.1 %collective-permute-start.32 = (bf16[1,72,1536]{2,1,0:T(8,128)(2,1)S(1)}, bf16[1,72,1536]{2,1,0:T(8,128)(2,1)S(1)}, u32[]{:S(2)}, u32[]{:S(2)}) collective-permute-start(bf16[1,72,1536]{2,1,0:T(8,128)(2,1)S(1)} %get-tuple-element.196), channel_id=1, source_target_pairs={{0,16},{2,18},{4,20},{6,22},{8,24},{10,26},{12,28},{14,30},{16,0},... | collective-permute-start | bytes 663560 | tf_op jit(solution)/shard_map/ppermute | solution.py:644
  232.8 15.3 %collective-permute-start.36 = (bf16[1,72,768]{2,1,0:T(8,128)(2,1)S(1)}, bf16[1,72,768]{2,1,0:T(8,128)(2,1)S(1)}, u32[]{:S(2)}, u32[]{:S(2)}) collective-permute-start(bf16[1,72,768]{2,1,0:T(8,128)(2,1)S(1)} %get-tuple-element.201), channel_id=1, source_target_pairs={{0,16},{2,18},{4,20},{6,22},{8,24},{10,26},{12,28},{14,30},{16,0},... | collective-permute-start | bytes 331784 | tf_op jit(solution)/shard_map/ppermute | solution.py:644
  (64 other events, 241.0 us)
